TPU v7x, 512 devices: a whole 4x8x8 slice. The times are simulated.
512 devices in a mesh: pipe: 16 (over z_lo, x), expert: 32 (over z_hi, y, core).
Axes of the slice: x: 4, y: 8, z: 8 (z_hi: 2, z_lo: 4; z = z_hi * 4 + z_lo), core: 2. Of those that a mesh axis runs over, the one named last changes fastest.
Arguments:
- stream_a: bfloat16 [16, 256, 3584], P('pipe', 'expert'), may hold values from -6 to 6
- stream_b: bfloat16 [16, 256, 3584], P('pipe', 'expert'), may hold values from -6 to 6
- routes: int32 [2, 2, 16, 256, 2], P(None, None, 'pipe', 'expert'), may hold values from 0 to 3, all different within a row; in each aligned block of 8 rows (0 to 7, 8 to 15, ..., all dimensions but the last counted through in order) at most 4 rows name the same one
- up_weight: bfloat16 [2, 16, 3584, 4096], P(None, 'pipe', None, 'expert'), as said below
- down_weight: bfloat16 [2, 16, 4096, 3584], P(None, 'pipe', 'expert'), as said below
- router_weight: bfloat16 [2, 16, 3584, 4], P(None, 'pipe'), as said below
Outputs:
- final_a: bfloat16 [16, 256, 3584], P('pipe', 'expert')
- final_b: bfloat16 [16, 256, 3584], P('pipe', 'expert')
- expert_load: float32 [16, 4], replicated
Inputs may be any that keep to these rules, and one draw needn't show every extreme that they name: `routes`: in each device's 8 rows of one tick, stream and section, every expert is named by exactly 4 rows, and each row names 2 different experts. up_weight[1, i] equals up_weight[0, 15 - i]. down_weight[1, i] equals down_weight[0, 15 - i]. router_weight[1, i] equals router_weight[0, 15 - i].
All inputs are finite; a program needn't handle non-finite values.
Results may differ from a plain program's by a relative error of at most 0.0065.
Values may be sent and summed in bfloat16 or wider, within the bound.
A program may use at most 64 MiB of HBM per device.

v0:
```python
import jax
import jax.numpy as jnp
from jax import lax
from jax.sharding import PartitionSpec as P

TICKS = 2


EPS = 1e-06


def from_behind(array, axis, by):
    length = lax.axis_size(axis)
    return lax.ppermute(array, axis, [(i, (i + by) % length) for i in range(length)])


def normalize(section_rows):
    widened = section_rows.astype(jnp.float32)
    return (widened * lax.rsqrt(jnp.mean(widened * widened, axis=-1, keepdims=True) + EPS)).astype(
        jnp.bfloat16
    )


def routing(normed, router, picked):
    experts = router.shape[-1]
    affinity = jax.nn.sigmoid(jnp.dot(normed, router, preferred_element_type=jnp.float32))
    member = (picked[:, :, None] == jnp.arange(experts, dtype=jnp.int32)[None, None, :]).astype(
        jnp.float32
    )
    chosen = jnp.sum(member * affinity[:, None, :], axis=2)
    shares = chosen / jnp.sum(chosen, axis=1, keepdims=True)
    weights = jnp.sum(shares[:, :, None] * member, axis=1)
    selected = jnp.sum(member, axis=1)
    return (weights, selected)


def prepare(section_rows, router, picked, group_size):
    normed = normalize(section_rows)
    weights, selected = routing(normed, router, picked)
    experts = router.shape[-1]
    capacity = section_rows.shape[0] * picked.shape[1] // experts
    before = jnp.cumsum(selected, axis=0) - selected
    slot_match = (
        before.T[:, None, :] == jnp.arange(capacity, dtype=jnp.float32)[None, :, None]
    ).astype(jnp.float32)
    placing = selected.T[:, None, :] * slot_match
    packed = jnp.einsum(
        "ecr,rd->ecd", placing.astype(jnp.bfloat16), normed, preferred_element_type=jnp.float32
    ).astype(jnp.bfloat16)
    features = packed.shape[2]
    outgoing = jnp.broadcast_to(packed[:, None], (experts, group_size, capacity, features)).reshape(
        experts * group_size, capacity, features
    )
    return (outgoing, placing * weights.T[:, None, :], jnp.sum(weights, axis=0))


def expert_rows(arrived, lift_weight, lower_weight):
    sources, slot_count, features = arrived.shape
    hidden = jax.nn.silu(
        jnp.dot(
            arrived.reshape(sources * slot_count, features),
            lift_weight,
            preferred_element_type=jnp.float32,
        )
    ).astype(jnp.bfloat16)
    partial_value = jnp.dot(hidden, lower_weight, preferred_element_type=jnp.float32).astype(
        jnp.bfloat16
    )
    return partial_value.reshape(sources, slot_count, features)


def finish(section_rows, returned, scaled, experts):
    sources, slot_count, features = returned.shape
    summed = (
        returned.reshape(experts, sources // experts, slot_count, features)
        .astype(jnp.float32)
        .sum(axis=1)
    )
    mixture = jnp.einsum("ecr,ecd->rd", scaled, summed, precision=lax.Precision.HIGHEST)
    return (section_rows.astype(jnp.float32) + mixture).astype(jnp.bfloat16)


def send_apart(outgoing, lift_weight, lower_weight):
    return lax.all_to_all(
        expert_rows(
            lax.all_to_all(outgoing, "expert", split_axis=0, concat_axis=0, tiled=True),
            lift_weight,
            lower_weight,
        ),
        "expert",
        split_axis=0,
        concat_axis=0,
        tiled=True,
    )


def shards(stream_a, stream_b, routes, up_weight, down_weight, router_weight):
    experts = router_weight.shape[-1]
    group_size = lax.axis_size("expert") // experts
    current = [stream_a[0], stream_b[0]]
    masses = [jnp.zeros((experts,), jnp.float32), jnp.zeros((experts,), jnp.float32)]
    for step_index in range(TICKS):
        if step_index > 0:
            current = [from_behind(current[0], "pipe", 1), from_behind(current[1], "pipe", -1)]
        prepared = [
            prepare(
                current[stream], router_weight[stream, 0], routes[step_index, stream, 0], group_size
            )
            for stream in range(2)
        ]
        returned = [
            send_apart(prepared[stream][0], up_weight[stream, 0], down_weight[stream, 0])
            for stream in range(2)
        ]
        current = [
            finish(current[stream], returned[stream], prepared[stream][1], experts)
            for stream in range(2)
        ]
        masses = [masses[stream] + prepared[stream][2] for stream in range(2)]
    layers = lax.axis_size("pipe")
    position = lax.axis_index("pipe")
    ladder = jnp.arange(layers, dtype=jnp.int32)
    own_row = (ladder == position).astype(jnp.float32)[:, None]
    mirror_row = (ladder == layers - 1 - position).astype(jnp.float32)[:, None]
    totals = lax.psum((masses[0], masses[1]), "expert")
    spread_table = own_row * totals[0][None, :] + mirror_row * totals[1][None, :]
    load_table = lax.psum(spread_table, "pipe")
    tokens_total = 2 * TICKS * current[0].shape[0] * lax.axis_size("expert")
    return (current[0][None], current[1][None], load_table / tokens_total)


def solution(mesh):
    return jax.shard_map(
        shards,
        mesh=mesh,
        in_specs=(
            P("pipe", "expert", None),
            P("pipe", "expert", None),
            P(None, None, "pipe", "expert", None),
            P(None, "pipe", None, "expert"),
            P(None, "pipe", "expert", None),
            P(None, "pipe", None, None),
        ),
        out_specs=(P("pipe", "expert", None), P("pipe", "expert", None), P()),
        check_vma=False,
    )
```

profile of v0, /device:TPU:256, one launch (start us, length us, event | category | flops | bytes accessed | tf_op | source)
XLA Modules:
  0.0 421.3 jit_solution(10804050746090665796)
XLA Ops:
  0.7 0.8 slice_bitcast_fusion
  1.4 1.0 fusion.50
  2.4 1.0 fusion.21
  3.8 1.0 convolution_convert_fusion.7
  4.8 1.2 broadcast_in_dim.12
  6.0 12.6 %all-to-all-start = ((bf16[32,4,3584]{2,1,0:T(4,128)(2,1)}), bf16[32,4,3584]{2,1,0:T(4,128)(2,1)S(1)}, u32[]{:S(2)}, u32[]{:S(2)}) async-start(bf16[32,4,3584]{2,1,0:T(4,128)(2,1)} %bitcast.8), calls=%async_computation | async-start | bytes 1835008 | tf_op jit(solution)/shard_map/all_to_all | solution.py:86
  19.6 23.8 %all-to-all-done = bf16[32,4,3584]{2,1,0:T(4,128)(2,1)S(1)} async-done(((bf16[32,4,3584]{2,1,0:T(4,128)(2,1)}), bf16[32,4,3584]{2,1,0:T(4,128)(2,1)S(1)}, u32[]{:S(2)}, u32[]{:S(2)}) %all-to-all-start) | async-done | bytes 917536 | tf_op jit(solution)/shard_map/all_to_all | solution.py:86
  43.5 1.2 broadcast_in_dim.15
  44.7 9.7 %all-to-all-start.4 = ((bf16[32,4,3584]{2,1,0:T(4,128)(2,1)}), bf16[32,4,3584]{2,1,0:T(4,128)(2,1)}, u32[]{:S(2)}, u32[]{:S(2)}) async-start(bf16[32,4,3584]{2,1,0:T(4,128)(2,1)} %bitcast.30), calls=%async_computation.4 | async-start | bytes 1835008 | tf_op jit(solution)/shard_map/all_to_all | solution.py:86
  54.4 1.7 reshape.215
  56.1 2.9 convolution_convert_fusion.3
  59.0 2.5 reshape.216
  61.5 17.7 %all-to-all-done.4 = bf16[32,4,3584]{2,1,0:T(4,128)(2,1)} async-done(((bf16[32,4,3584]{2,1,0:T(4,128)(2,1)}), bf16[32,4,3584]{2,1,0:T(4,128)(2,1)}, u32[]{:S(2)}, u32[]{:S(2)}) %all-to-all-start.4) | async-done | bytes 917536 | tf_op jit(solution)/shard_map/all_to_all | solution.py:86
  79.2 9.7 %all-to-all-start.1 = ((bf16[32,4,3584]{2,1,0:T(4,128)(2,1)}), bf16[32,4,3584]{2,1,0:T(4,128)(2,1)}, u32[]{:S(2)}, u32[]{:S(2)}) async-start(bf16[32,4,3584]{2,1,0:T(4,128)(2,1)} %reshape.216), calls=%async_computation.1 | async-start | bytes 1835008 | tf_op jit(solution)/shard_map/all_to_all | solution.py:84
  88.8 1.7 reshape.221
  90.5 2.9 convolution_convert_fusion.1
  93.4 2.5 reshape.222
  95.9 17.7 %all-to-all-done.1 = bf16[32,4,3584]{2,1,0:T(4,128)(2,1)} async-done(((bf16[32,4,3584]{2,1,0:T(4,128)(2,1)}), bf16[32,4,3584]{2,1,0:T(4,128)(2,1)}, u32[]{:S(2)}, u32[]{:S(2)}) %all-to-all-start.1) | async-done | bytes 917536 | tf_op jit(solution)/shard_map/all_to_all | solution.py:84
  113.6 9.2 %all-to-all-start.5 = ((bf16[32,4,3584]{2,1,0:T(4,128)(2,1)}), bf16[32,4,3584]{2,1,0:T(4,128)(2,1)S(1)}, u32[]{:S(2)}, u32[]{:S(2)}) async-start(bf16[32,4,3584]{2,1,0:T(4,128)(2,1)} %reshape.222), calls=%async_computation.5 | async-start | bytes 1835008 | tf_op jit(solution)/shard_map/all_to_all | solution.py:84
  122.8 1.6 convert_reduce_fusion.3
  124.4 0.5 fusion.7
  124.9 3.4 collective-permute-start
  128.3 19.3 %all-to-all-done.5 = bf16[32,4,3584]{2,1,0:T(4,128)(2,1)S(1)} async-done(((bf16[32,4,3584]{2,1,0:T(4,128)(2,1)}), bf16[32,4,3584]{2,1,0:T(4,128)(2,1)S(1)}, u32[]{:S(2)}, u32[]{:S(2)}) %all-to-all-start.5) | async-done | bytes 917536 | tf_op jit(solution)/shard_map/all_to_all | solution.py:84
  148.0 0.5 fusion.5
  148.5 7.2 %collective-permute-start.1 = (bf16[8,3584]{1,0:T(8,128)(2,1)S(1)}, bf16[8,3584]{1,0:T(8,128)(2,1)S(1)}, u32[]{:S(2)}, u32[]{:S(2)}) collective-permute-start(bf16[8,3584]{1,0:T(8,128)(2,1)S(1)} %fusion.5), channel_id=1, source_target_pairs={{0,480},{32,0},{64,32},{96,64},{128,96},{160,128},{192,160},{224,1... | collective-permute-start | bytes 172040 | tf_op jit(solution)/shard_map/ppermute | solution.py:14
  155.8 1.6 collective-permute-done.1
  158.8 1.2 broadcast_in_dim.16
  159.9 9.0 %all-to-all-start.6 = ((bf16[32,4,3584]{2,1,0:T(4,128)(2,1)}), bf16[32,4,3584]{2,1,0:T(4,128)(2,1)S(1)}, u32[]{:S(2)}, u32[]{:S(2)}) async-start(bf16[32,4,3584]{2,1,0:T(4,128)(2,1)} %bitcast.174), calls=%async_computation.6 | async-start | bytes 1835008 | tf_op jit(solution)/shard_map/all_to_all | solution.py:86
  169.3 24.3 %all-to-all-done.6 = bf16[32,4,3584]{2,1,0:T(4,128)(2,1)S(1)} async-done(((bf16[32,4,3584]{2,1,0:T(4,128)(2,1)}), bf16[32,4,3584]{2,1,0:T(4,128)(2,1)S(1)}, u32[]{:S(2)}, u32[]{:S(2)}) %all-to-all-start.6) | async-done | bytes 917536 | tf_op jit(solution)/shard_map/all_to_all | solution.py:86
  193.7 1.2 broadcast_in_dim.13
  194.9 9.6 %all-to-all-start.2 = ((bf16[32,4,3584]{2,1,0:T(4,128)(2,1)}), bf16[32,4,3584]{2,1,0:T(4,128)(2,1)}, u32[]{:S(2)}, u32[]{:S(2)}) async-start(bf16[32,4,3584]{2,1,0:T(4,128)(2,1)} %bitcast.175), calls=%async_computation.2 | async-start | bytes 1835008 | tf_op jit(solution)/shard_map/all_to_all | solution.py:86
  204.5 1.7 reshape.224
  206.2 2.9 convolution_convert_fusion
  209.1 2.5 reshape.225
  211.6 17.5 %all-to-all-done.2 = bf16[32,4,3584]{2,1,0:T(4,128)(2,1)} async-done(((bf16[32,4,3584]{2,1,0:T(4,128)(2,1)}), bf16[32,4,3584]{2,1,0:T(4,128)(2,1)}, u32[]{:S(2)}, u32[]{:S(2)}) %all-to-all-start.2) | async-done | bytes 917536 | tf_op jit(solution)/shard_map/all_to_all | solution.py:86
  229.1 9.9 %all-to-all-start.7 = ((bf16[32,4,3584]{2,1,0:T(4,128)(2,1)}), bf16[32,4,3584]{2,1,0:T(4,128)(2,1)}, u32[]{:S(2)}, u32[]{:S(2)}) async-start(bf16[32,4,3584]{2,1,0:T(4,128)(2,1)} %reshape.225), calls=%async_computation.7 | async-start | bytes 1835008 | tf_op jit(solution)/shard_map/all_to_all | solution.py:84
  239.0 1.7 reshape.218
  240.6 2.9 convolution_convert_fusion.2
  243.5 2.5 reshape.219
  246.0 17.7 %all-to-all-done.7 = bf16[32,4,3584]{2,1,0:T(4,128)(2,1)} async-done(((bf16[32,4,3584]{2,1,0:T(4,128)(2,1)}), bf16[32,4,3584]{2,1,0:T(4,128)(2,1)}, u32[]{:S(2)}, u32[]{:S(2)}) %all-to-all-start.7) | async-done | bytes 917536 | tf_op jit(solution)/shard_map/all_to_all | solution.py:84
  263.7 9.0 %all-to-all-start.3 = ((bf16[32,4,3584]{2,1,0:T(4,128)(2,1)}), bf16[32,4,3584]{2,1,0:T(4,128)(2,1)S(1)}, u32[]{:S(2)}, u32[]{:S(2)}) async-start(bf16[32,4,3584]{2,1,0:T(4,128)(2,1)} %reshape.219), calls=%async_computation.3 | async-start | bytes 1835008 | tf_op jit(solution)/shard_map/all_to_all | solution.py:84
  272.8 99.6 %all-reduce = (f32[4]{0:T(128)S(1)}, f32[4]{0:T(128)S(1)}) all-reduce(f32[4]{0:T(128)S(1)} %add.101, f32[4]{0:T(128)S(1)} %add.100), channel_id=1, replica_groups=mesh['pipe'=16,'expert'=32] {'expert'}, use_global_device_ids=true, to_apply=%region_33.34 | all-reduce | flops 8 | bytes 64 | tf_op jit(solution)/shard_map/psum | solution.py:125
  372.4 44.0 %psum.23 = f32[16,4]{0,1:T(4,128)S(1)} all-reduce(f32[16,4]{0,1:T(4,128)S(1)} %multiply_add_fusion), channel_id=1, replica_groups=mesh['pipe'=16,'expert'=32] {'pipe'}, use_global_device_ids=true, to_apply=%region_34.35 | all-reduce | flops 64 | bytes 512 | tf_op jit(solution)/shard_map/psum | solution.py:127
  416.5 0.6 broadcast_multiply_fusion
  417.0 1.6 convert_reduce_fusion
  418.7 0.4 convert_reduce_fusion.2
  419.1 1.1 fusion.9
  420.2 1.1 fusion.8
  (55 shorter events, 3.6 us)
Async XLA Ops:
  0.6 18.2 %copy-start.5 = (bf16[2,1,3584,4]{2,3,1,0:T(4,128)(2,1)S(1)}, bf16[2,1,3584,4]{2,3,1,0:T(4,128)(2,1)}, u32[]{:S(2)}) copy-start(bf16[2,1,3584,4]{2,3,1,0:T(4,128)(2,1)} %param.11) | copy-start | bytes 172036
  0.6 18.0 %copy-start.4 = (bf16[1,8,3584]{2,1,0:T(8,128)(2,1)S(1)}, bf16[1,8,3584]{2,1,0:T(8,128)(2,1)}, u32[]{:S(2)}) copy-start(bf16[1,8,3584]{2,1,0:T(8,128)(2,1)} %param.7) | copy-start | bytes 172036
  6.0 37.5 %all-to-all-start = ((bf16[32,4,3584]{2,1,0:T(4,128)(2,1)}), bf16[32,4,3584]{2,1,0:T(4,128)(2,1)S(1)}, u32[]{:S(2)}, u32[]{:S(2)}) async-start(bf16[32,4,3584]{2,1,0:T(4,128)(2,1)} %bitcast.8), calls=%async_computation | async-start | bytes 1835008 | tf_op jit(solution)/shard_map/all_to_all | solution.py:86
  43.5 1.2 copy-start.1
  44.7 11.4 %copy-start = (bf16[2,1,128,3584]{3,2,1,0:T(8,128)(2,1)S(1)}, bf16[2,1,128,3584]{3,2,1,0:T(8,128)(2,1)}, u32[]{:S(2)}) copy-start(bf16[2,1,128,3584]{3,2,1,0:T(8,128)(2,1)} %param.10) | copy-start | bytes 5505028
  44.7 34.5 %all-to-all-start.4 = ((bf16[32,4,3584]{2,1,0:T(4,128)(2,1)}), bf16[32,4,3584]{2,1,0:T(4,128)(2,1)}, u32[]{:S(2)}, u32[]{:S(2)}) async-start(bf16[32,4,3584]{2,1,0:T(4,128)(2,1)} %bitcast.30), calls=%async_computation.4 | async-start | bytes 1835008 | tf_op jit(solution)/shard_map/all_to_all | solution.py:86
  79.2 34.4 %all-to-all-start.1 = ((bf16[32,4,3584]{2,1,0:T(4,128)(2,1)}), bf16[32,4,3584]{2,1,0:T(4,128)(2,1)}, u32[]{:S(2)}, u32[]{:S(2)}) async-start(bf16[32,4,3584]{2,1,0:T(4,128)(2,1)} %reshape.216), calls=%async_computation.1 | async-start | bytes 1835008 | tf_op jit(solution)/shard_map/all_to_all | solution.py:84
  95.9 28.5 %copy-start.3 = (bf16[1,8,3584]{2,1,0:T(8,128)(2,1)S(1)}, bf16[1,8,3584]{2,1,0:T(8,128)(2,1)}, u32[]{:S(2)}) copy-start(bf16[1,8,3584]{2,1,0:T(8,128)(2,1)} %param.6) | copy-start | bytes 172036
  113.6 34.0 %all-to-all-start.5 = ((bf16[32,4,3584]{2,1,0:T(4,128)(2,1)}), bf16[32,4,3584]{2,1,0:T(4,128)(2,1)S(1)}, u32[]{:S(2)}, u32[]{:S(2)}) async-start(bf16[32,4,3584]{2,1,0:T(4,128)(2,1)} %reshape.222), calls=%async_computation.5 | async-start | bytes 1835008 | tf_op jit(solution)/shard_map/all_to_all | solution.py:84
  124.9 30.8 %collective-permute-start = (bf16[8,3584]{1,0:T(8,128)(2,1)S(1)}, bf16[8,3584]{1,0:T(8,128)(2,1)S(1)}, u32[]{:S(2)}, u32[]{:S(2)}) collective-permute-start(bf16[8,3584]{1,0:T(8,128)(2,1)S(1)} %fusion.7), channel_id=1, source_target_pairs={{0,32},{32,64},{64,96},{96,128},{128,160},{160,192},{192,224},{224... | collective-permute-start | bytes 172040 | tf_op jit(solution)/shard_map/ppermute | solution.py:14
  148.5 9.0 %collective-permute-start.1 = (bf16[8,3584]{1,0:T(8,128)(2,1)S(1)}, bf16[8,3584]{1,0:T(8,128)(2,1)S(1)}, u32[]{:S(2)}, u32[]{:S(2)}) collective-permute-start(bf16[8,3584]{1,0:T(8,128)(2,1)S(1)} %fusion.5), channel_id=1, source_target_pairs={{0,480},{32,0},{64,32},{96,64},{128,96},{160,128},{192,160},{224,1... | collective-permute-start | bytes 172040 | tf_op jit(solution)/shard_map/ppermute | solution.py:14
  159.9 33.7 %all-to-all-start.6 = ((bf16[32,4,3584]{2,1,0:T(4,128)(2,1)}), bf16[32,4,3584]{2,1,0:T(4,128)(2,1)S(1)}, u32[]{:S(2)}, u32[]{:S(2)}) async-start(bf16[32,4,3584]{2,1,0:T(4,128)(2,1)} %bitcast.174), calls=%async_computation.6 | async-start | bytes 1835008 | tf_op jit(solution)/shard_map/all_to_all | solution.py:86
  193.7 1.2 copy-start.2
  194.9 34.2 %all-to-all-start.2 = ((bf16[32,4,3584]{2,1,0:T(4,128)(2,1)}), bf16[32,4,3584]{2,1,0:T(4,128)(2,1)}, u32[]{:S(2)}, u32[]{:S(2)}) async-start(bf16[32,4,3584]{2,1,0:T(4,128)(2,1)} %bitcast.175), calls=%async_computation.2 | async-start | bytes 1835008 | tf_op jit(solution)/shard_map/all_to_all | solution.py:86
  229.1 34.7 %all-to-all-start.7 = ((bf16[32,4,3584]{2,1,0:T(4,128)(2,1)}), bf16[32,4,3584]{2,1,0:T(4,128)(2,1)}, u32[]{:S(2)}, u32[]{:S(2)}) async-start(bf16[32,4,3584]{2,1,0:T(4,128)(2,1)} %reshape.225), calls=%async_computation.7 | async-start | bytes 1835008 | tf_op jit(solution)/shard_map/all_to_all | solution.py:84
  263.7 154.9 %all-to-all-start.3 = ((bf16[32,4,3584]{2,1,0:T(4,128)(2,1)}), bf16[32,4,3584]{2,1,0:T(4,128)(2,1)S(1)}, u32[]{:S(2)}, u32[]{:S(2)}) async-start(bf16[32,4,3584]{2,1,0:T(4,128)(2,1)} %reshape.219), calls=%async_computation.3 | async-start | bytes 1835008 | tf_op jit(solution)/shard_map/all_to_all | solution.py:84
where the time goes:
time: 423 us; the launch traced here: 421 us
  blocking collectives  144 us (34%)
  waiting for transfers between devices  140 us (33%)
  starting transfers between devices  89.3 us (21%)
  local copies, waits for them, and re-layouts  22.3 us (5%)
  matrix products  18 us (4%)
  other arithmetic  7.51 us (2%)
    psum x1, blocking collectives, shards(): totals = lax.psum((masses[0], masses[1]), 'expert')  99.6 us
    all_to_all x4, waiting for transfers between devices, send_apart(): lax.all_to_all(outgoing, 'expert', split_axis=0, concat_axis=0, tiled=True)  83.3 us
    all_to_all x4, waiting for transfers between devices, send_apart(): lax.all_to_all(expert_rows(lax.all_to_all(outgoing, 'expert', split_axis=...  54.7 us
    psum x1, blocking collectives, shards(): load_table = lax.psum(spread_table, 'pipe')  44 us
    all_to_all x4, starting transfers between devices, send_apart(): lax.all_to_all(outgoing, 'expert', split_axis=0, concat_axis=0, tiled=True)  40.9 us
    all_to_all x4, starting transfers between devices, send_apart(): lax.all_to_all(expert_rows(lax.all_to_all(outgoing, 'expert', split_axis=...  37.7 us
    dot_general x4, matrix products, expert_rows(): jnp.dot(hidden, lower_weight, preferred_element_type=jnp.float32)  11.5 us
    ppermute x2, starting transfers between devices, from_behind(): lax.ppermute(array, axis, [(i, (i + by) % length) for i in range(length)])  10.6 us
  transfers between devices with their start and end apart: 10, of which 8 were waited for; matrix products, arithmetic and copies ran while one was open for 8% of the time, Pallas kernels for 0%

commit v1 on v0

v1 whole, which is shorter than its diff:
```python
import jax
import jax.numpy as jnp
from jax import lax
from jax.experimental import pallas as pl
from jax.experimental.pallas import tpu as pltpu
from jax.sharding import PartitionSpec as P

TICKS = 2
EPS = 1e-06
QUARTERS = 4
CAP = 4
SIDE = 8
MESH = pl.DeviceIdType.MESH

Z_OUT, Y_OWN, Y_PEER, Y_BACK, Z_BACK, RELAY = range(6)
BLOCK = 16


def kernel(
    sa, sb, routes, router, up, down,
    out_a, out_b, out_load,
    u, w, tx, zrx, rx, back, crx, ztx, zc, xtx, xr, mtx, mrx,
    send, recv, wlocal, wsend, wrecv, msend, mrecv,
):
    quarter = u.shape[1]
    features = QUARTERS * quarter
    pipe = lax.axis_index("pipe")
    ex = lax.axis_index("expert")
    zh = ex // 16
    y = (ex // 2) % SIDE
    core = ex % 2
    sibling = {"expert": ex + 1 - 2 * core}
    zpeer = {"expert": (1 - zh) * 16 + y * 2 + core}

    def chip_y(to):
        return {"expert": zh * 16 + to * 2 + core}

    def step_y(i):
        return lax.rem(y + jnp.where(i % 2 == 0, i // 2 + 1, SIDE - 1 - i // 2), SIDE)

    px, pz = pipe % 4, pipe // 4
    x_mates = [{"pipe": pz * 4 + (px + k) % 4} for k in range(1, 4)]
    z_mates = [{"pipe": ((pz + k) % 4) * 4 + px} for k in range(1, 4)]
    ahead = {"pipe": (pipe + 1) % 16}
    behind = {"pipe": (pipe + 15) % 16}

    def weight_parts(s, which):
        if which == 0:
            return [
                (
                    up.at[s, 0, pl.ds(q * quarter, quarter), :],
                    u.at[s, :, pl.ds(pl.multiple_of(q * 256 + core * 128, 128), 128)],
                )
                for q in range(QUARTERS)
            ]
        return [(down.at[s, 0], w.at[s, pl.ds(pl.multiple_of(core * 128, 128), 128), :])]

    for s in range(2):
        for which in range(2):
            for src, dst in weight_parts(s, which):
                pltpu.make_async_copy(src, dst, wlocal.at[s, which]).start()

    barrier = pltpu.get_barrier_semaphore()

    def greet(device):
        pl.semaphore_signal(barrier, inc=1, device_id=device, device_id_type=MESH)

    for device in [sibling, zpeer, ahead, behind] + x_mates + z_mates:
        greet(device)

    @pl.loop(0, SIDE - 1)
    def _(i):
        greet(chip_y(step_y(i)))

    pl.semaphore_wait(barrier, 4 + 6 + SIDE - 1)

    def remote(src, dst, t, s, kind, device):
        return pltpu.make_async_remote_copy(
            src_ref=src, dst_ref=dst, send_sem=send.at[t, s, kind],
            recv_sem=recv.at[t, s, kind], device_id=device, device_id_type=MESH,
        )

    def drain(ref, sem):
        pltpu.make_async_copy(ref, ref, sem).wait()

    def half_of_weight(s, which):
        return u.at[s, :, pl.ds(0, 512)] if which == 0 else w.at[s, pl.ds(0, 128), :]

    def send_weights(s):
        for which in range(2):
            for src, dst in weight_parts(s, which):
                pltpu.make_async_remote_copy(
                    src_ref=src, dst_ref=dst, send_sem=wsend.at[s, which],
                    recv_sem=wrecv.at[s, which], device_id=sibling, device_id_type=MESH,
                ).start()

    lane4 = lax.broadcasted_iota(jnp.int32, (8, 4), 1)
    low8 = (
        lax.broadcasted_iota(jnp.int32, (8, 8), 0) > lax.broadcasted_iota(jnp.int32, (8, 8), 1)
    ).astype(jnp.bfloat16)
    row64 = lax.broadcasted_iota(jnp.int32, (64, 4), 0)
    expert_hot = (row64 // BLOCK == lax.broadcasted_iota(jnp.int32, (64, 4), 1)).astype(
        jnp.bfloat16
    )
    row_t = lax.broadcasted_iota(jnp.int32, (64, 32), 0)
    col_t = lax.broadcasted_iota(jnp.int32, (64, 32), 1)
    same_quarter = (row_t // 4) % 4 == col_t // 8
    slot_t = (row_t % 4).astype(jnp.float32)

    def pieces(t, s):
        if t == 0:
            ref = sa if s == 0 else sb
            return [
                ref[0, :, q * quarter : (q + 1) * quarter].astype(jnp.float32)
                for q in range(QUARTERS)
            ]
        rows = xr[s].astype(jnp.float32)
        return [rows[q * 8 : (q + 1) * 8] for q in range(QUARTERS)]

    def prepare(t, s):
        x = pieces(t, s)
        total = sum(jnp.sum(part * part, axis=1, keepdims=True) for part in x)
        scale = lax.rsqrt(total / features + EPS)
        normed = [part * scale for part in x]
        normed4 = jnp.concatenate(normed, axis=0).astype(jnp.bfloat16)
        logits = sum(
            jnp.dot(
                normed[q].astype(jnp.bfloat16),
                router[s, 0, q * quarter : (q + 1) * quarter, :],
                preferred_element_type=jnp.float32,
            )
            for q in range(QUARTERS)
        )
        affinity = jax.nn.sigmoid(logits)
        picked = routes[t, s, 0]
        member = [(picked[:, j : j + 1] == lane4).astype(jnp.float32) for j in range(2)]
        chosen = [jnp.sum(m * affinity, axis=1, keepdims=True) for m in member]
        both = chosen[0] + chosen[1]
        gates = (chosen[0] / both) * member[0] + (chosen[1] / both) * member[1]
        selected = member[0] + member[1]
        before = jnp.dot(low8, selected.astype(jnp.bfloat16), preferred_element_type=jnp.float32)
        slot = jnp.where(selected > 0, before, -1.0)
        slot4 = jnp.concatenate([slot] * QUARTERS, axis=0).astype(jnp.bfloat16)
        slot_of = lax.dot_general(
            expert_hot, slot4, (((1,), (1,)), ((), ())), preferred_element_type=jnp.float32
        )
        place = jnp.where(same_quarter & (slot_of == slot_t), 1.0, 0.0).astype(jnp.bfloat16)
        tx[t, s] = jnp.dot(place, normed4, preferred_element_type=jnp.float32).astype(jnp.bfloat16)
        return gates, slot

    def block(index):
        return pl.ds(pl.multiple_of(index * BLOCK, BLOCK), BLOCK)

    def dispatch(t, s):
        remote(
            tx.at[t, s, pl.ds(pl.multiple_of((1 - zh) * 32, 32), 32)], zrx.at[t, s],
            t, s, Z_OUT, zpeer,
        ).start()

        @pl.loop(0, SIDE - 1)
        def _(i):
            to = step_y(i)
            remote(
                tx.at[t, s, block(zh * 2 + to // 4)], rx.at[t, s, block(y * 2 + zh)],
                t, s, Y_OWN, chip_y(to),
            ).start()

        rx[t, s, block(y * 2 + zh)] = tx[t, s, block(zh * 2 + y // 4)]

    def dispatch_peer(t, s):
        drain(zrx.at[t, s], recv.at[t, s, Z_OUT])

        @pl.loop(0, SIDE - 1)
        def _(i):
            to = step_y(i)
            remote(
                zrx.at[t, s, block(to // 4)], rx.at[t, s, block(y * 2 + 1 - zh)],
                t, s, Y_PEER, chip_y(to),
            ).start()

        rx[t, s, block(y * 2 + 1 - zh)] = zrx[t, s, block(y // 4)]

    def experts(t, s):
        for kind in (Y_OWN, Y_PEER):
            drain(rx.at[t, s, pl.ds(0, (SIDE - 1) * BLOCK)], recv.at[t, s, kind])
        if t == 0:
            drain(u.at[s, :, pl.ds(0, 512)], wlocal.at[s, 0])
            drain(u.at[s, :, pl.ds(0, 512)], wrecv.at[s, 0])
        arrived = rx[t, s]
        lower = lax.broadcasted_iota(jnp.int32, (16, 8, 256), 1) < 4
        lifted = [
            jnp.dot(
                arrived, u[s, :, q * 256 : (q + 1) * 256], preferred_element_type=jnp.float32
            ).reshape(16, 2, 8, 256)
            for q in range(QUARTERS)
        ]
        part = jnp.where(lower, lifted[0][:, 0], lifted[1][:, 0]) + jnp.where(
            lower, lifted[2][:, 1], lifted[3][:, 1]
        )
        part = part.reshape(128, 256)
        lower2 = lax.broadcasted_iota(jnp.int32, (128, 256), 0) % 8 < 4
        other = jnp.where(lower2, pltpu.roll(part, 124, 0), pltpu.roll(part, 4, 0))
        hidden = jax.nn.silu(part + other).astype(jnp.bfloat16)
        if t == 0:
            drain(w.at[s, pl.ds(0, 128), :], wlocal.at[s, 1])
            drain(w.at[s, pl.ds(0, 128), :], wrecv.at[s, 1])
        lower3 = lax.broadcasted_iota(jnp.int32, (128, quarter), 0) % 8 < 4
        halves = []
        for h in range(2):
            two = [
                jnp.dot(
                    hidden, w[s, :, q * quarter : (q + 1) * quarter],
                    preferred_element_type=jnp.float32,
                )
                for q in (2 * h, 2 * h + 1)
            ]
            halves.append(jnp.where(lower3, two[0], two[1]).reshape(16, 1, 8, quarter))
        back[t, s] = (
            jnp.concatenate(halves, axis=1).reshape(256, quarter).astype(jnp.bfloat16)
        )

        def pair(index):
            return pl.ds(pl.multiple_of(index * 32, 32), 32)

        @pl.loop(0, SIDE - 1)
        def _(i):
            to = step_y(i)
            remote(
                back.at[t, s, pair(to)], crx.at[t, s, pair(y)], t, s, Y_BACK, chip_y(to)
            ).start()

        crx[t, s, pair(y)] = back[t, s, pair(y)]

    def sum_back(t, s):
        drain(crx.at[t, s, pl.ds(0, (SIDE - 1) * 32)], recv.at[t, s, Y_BACK])

        def over_line(zsrc, h):
            return sum(
                crx[t, s, block((h * 4 + k) * 2 + zsrc)].astype(jnp.float32) for k in range(4)
            )

        for h in range(2):
            ztx[t, s, h * BLOCK : (h + 1) * BLOCK] = over_line(1 - zh, h).astype(jnp.bfloat16)
        remote(ztx.at[t, s], zc.at[t, s], t, s, Z_BACK, zpeer).start()
        return [over_line(zh, h) for h in range(2)]

    def finish(t, s, own, gates, slot):
        drain(zc.at[t, s], recv.at[t, s, Z_BACK])
        other = [zc[t, s, h * BLOCK : (h + 1) * BLOCK].astype(jnp.float32) for h in range(2)]
        x = pieces(t, s)
        first = zh == 0
        terms = []
        for h in range(2):
            for sums, low in ((own[h], first), (other[h], jnp.logical_not(first))):
                gate = jnp.where(low, gates[:, h : h + 1], gates[:, 2 + h : 3 + h])
                place = jnp.where(low, slot[:, h : h + 1], slot[:, 2 + h : 3 + h])
                for c in range(CAP):
                    terms.append((sums, c, jnp.where(place == c, gate, 0.0)))
        rows = []
        for q in range(QUARTERS):
            total = x[q]
            for sums, c, factor in terms:
                total = total + factor * sums[q * 4 + c : q * 4 + c + 1, :]
            rows.append(total)
        if t + 1 < TICKS:
            xtx[s] = jnp.concatenate(rows, axis=0).astype(jnp.bfloat16)
            remote(xtx.at[s], xr.at[s], t, s, RELAY, ahead if s == 0 else behind).start()
        else:
            ref = out_a if s == 0 else out_b
            for q in range(QUARTERS):
                ref[0, :, q * quarter : (q + 1) * quarter] = rows[q].astype(jnp.bfloat16)

    y_mates = [chip_y(lax.rem(y + k, SIDE)) for k in range(1, SIDE)]
    rounds = [[sibling], y_mates, [zpeer], x_mates, z_mates]

    def mass_send(k):
        for i, device in enumerate(rounds[k]):
            pltpu.make_async_remote_copy(
                src_ref=mtx.at[k], dst_ref=mrx.at[k, i], send_sem=msend.at[k],
                recv_sem=mrecv.at[k], device_id=device, device_id_type=MESH,
            ).start()

    def mass_take(k):
        count = len(rounds[k])
        drain(mrx.at[k, pl.ds(0, count)], mrecv.at[k])
        return sum((mrx[k, i] for i in range(count)), mtx[k])

    def mass_step(k):
        mtx[k + 1] = mass_take(k)
        mass_send(k + 1)

    masses = [None, None]
    for t in range(TICKS):
        routed = [None, None]
        for s in range(2):
            if t > 0:
                drain(xr.at[s], recv.at[t - 1, s, RELAY])
            routed[s] = prepare(t, s)
            dispatch(t, s)
            mass = jnp.sum(routed[s][0], axis=0, keepdims=True)
            masses[s] = mass if t == 0 else masses[s] + mass
            if t == 0:
                send_weights(s)
        if t == TICKS - 1:
            row = lax.broadcasted_iota(jnp.int32, (16, 4), 0)
            table = jnp.where(row == pipe, masses[0], 0.0) + jnp.where(
                row == 15 - pipe, masses[1], 0.0
            )
            mtx[0] = jnp.zeros_like(mtx[0])
            mtx[0, :, 0:4] = table
            mass_send(0)
        last = t == TICKS - 1
        for s in range(2):
            dispatch_peer(t, s)
        for s in range(2):
            if last:
                mass_step(s)
            experts(t, s)
        own = []
        for s in range(2):
            if last:
                mass_step(2 + s)
            own.append(sum_back(t, s))
        for s in range(2):
            finish(t, s, own[s], *routed[s])
    out_load[...] = mass_take(4)[:, 0:4] / (2 * TICKS * 8 * 32)

    for s in range(2):
        for which in range(2):
            drain(half_of_weight(s, which), wsend.at[s, which])
    for k in range(5):
        drain(mrx.at[k, pl.ds(0, len(rounds[k]))], msend.at[k])
    for t in range(TICKS):
        for s in range(2):
            drain(zrx.at[t, s], send.at[t, s, Z_OUT])
            for kind in (Y_OWN, Y_PEER):
                drain(rx.at[t, s, pl.ds(0, (SIDE - 1) * BLOCK)], send.at[t, s, kind])
            drain(crx.at[t, s, pl.ds(0, (SIDE - 1) * 32)], send.at[t, s, Y_BACK])
            drain(zc.at[t, s], send.at[t, s, Z_BACK])
            if t + 1 < TICKS:
                drain(xr.at[s], send.at[t, s, RELAY])


def shards(stream_a, stream_b, routes, up_weight, down_weight, router_weight):
    features = stream_a.shape[2]
    quarter = features // QUARTERS
    vmem = pl.BlockSpec(memory_space=pltpu.VMEM)
    hbm = pl.BlockSpec(memory_space=pl.ANY)
    bf16, f32 = jnp.bfloat16, jnp.float32
    return pl.pallas_call(
        kernel,
        out_shape=(
            jax.ShapeDtypeStruct(stream_a.shape, bf16),
            jax.ShapeDtypeStruct(stream_b.shape, bf16),
            jax.ShapeDtypeStruct((16, 4), f32),
        ),
        in_specs=[vmem, vmem, vmem, vmem, hbm, hbm],
        out_specs=(vmem, vmem, vmem),
        scratch_shapes=[
            pltpu.VMEM((2, quarter, QUARTERS * 256), bf16),
            pltpu.VMEM((2, 256, features), bf16),
            pltpu.VMEM((TICKS, 2, 64, quarter), bf16),
            pltpu.VMEM((TICKS, 2, 32, quarter), bf16),
            pltpu.VMEM((TICKS, 2, 256, quarter), bf16),
            pltpu.VMEM((TICKS, 2, 256, quarter), bf16),
            pltpu.VMEM((TICKS, 2, 256, quarter), bf16),
            pltpu.VMEM((TICKS, 2, 32, quarter), bf16),
            pltpu.VMEM((TICKS, 2, 32, quarter), bf16),
            pltpu.VMEM((2, 32, quarter), bf16),
            pltpu.VMEM((2, 32, quarter), bf16),
            pltpu.VMEM((5, 16, 128), f32),
            pltpu.VMEM((5, SIDE - 1, 16, 128), f32),
            pltpu.SemaphoreType.DMA((TICKS, 2, 6)),
            pltpu.SemaphoreType.DMA((TICKS, 2, 6)),
            pltpu.SemaphoreType.DMA((2, 2)),
            pltpu.SemaphoreType.DMA((2, 2)),
            pltpu.SemaphoreType.DMA((2, 2)),
            pltpu.SemaphoreType.DMA((5,)),
            pltpu.SemaphoreType.DMA((5,)),
        ],
        compiler_params=pltpu.CompilerParams(
            collective_id=0, has_side_effects=True, vmem_limit_bytes=48 * 2**20
        ),
        name="relay",
    )(stream_a, stream_b, routes, router_weight, up_weight, down_weight)


def solution(mesh):
    return jax.shard_map(
        shards,
        mesh=mesh,
        in_specs=(
            P("pipe", "expert", None),
            P("pipe", "expert", None),
            P(None, None, "pipe", "expert", None),
            P(None, "pipe", None, "expert"),
            P(None, "pipe", "expert", None),
            P(None, "pipe", None, None),
        ),
        out_specs=(P("pipe", "expert", None), P("pipe", "expert", None), P()),
        check_vma=False,
    )
```

time: 423 us -> 120 us (0.28)
  the two profiles are of different devices: /device:TPU:256 before, /device:TPU:8 now
where the time goes in v1:
time: 120 us
  Pallas kernels  112 us (93%)
  local copies, waits for them, and re-layouts  7.39 us (6%)
    pallas_call x1, Pallas kernels, shards(): pl.pallas_call(kernel, out_shape=(jax.ShapeDtypeStruct(stream_a.shape, bf...  112 us
    unnamed x12, local copies, waits for them, and re-layouts  6.74 us

profile of v1, /device:TPU:8, one launch (start us, length us, event | category | flops | bytes accessed | tf_op | source)
XLA Modules:
  0.0 119.9 jit_solution(10018054194115049178)
XLA Ops:
  0.6 0.0 copy-start.3
  0.6 0.0 copy-start.2
  0.7 0.8 copy.9.routes
  1.5 1.7 %copy.10.router = bf16[2,1,3584,4]{3,2,1,0:T(8,128)(2,1)S(1)} copy(bf16[2,1,3584,4]{2,3,1,0:T(4,128)(2,1)} %param.11) | data formatting | bytes 114688 | tf_op args[5]
  3.2 0.0 copy-done.3
  3.2 0.0 copy-done.2
  3.2 0.0 copy-start
  3.2 1.5 %copy-done = bf16[2,1,3584,128]{3,2,1,0:T(8,128)(2,1)S(1)} copy-done((bf16[2,1,3584,128]{3,2,1,0:T(8,128)(2,1)S(1)}, bf16[2,1,3584,128]{3,2,1,0:T(8,128)(2,1)}, u32[]{:S(2)}) %copy-start) | copy-done | bytes 1835032
  4.7 0.0 copy-start.1
  4.7 1.5 %copy-done.1 = bf16[2,1,128,3584]{3,2,1,0:T(8,128)(2,1)S(1)} copy-done((bf16[2,1,128,3584]{3,2,1,0:T(8,128)(2,1)S(1)}, bf16[2,1,128,3584]{3,2,1,0:T(8,128)(2,1)}, u32[]{:S(2)}) %copy-start.1) | copy-done | bytes 1835032
  6.2 111.8 %relay.1 = (bf16[1,8,3584]{2,1,0:T(8,128)(2,1)S(1)}, bf16[1,8,3584]{2,1,0:T(8,128)(2,1)S(1)}, f32[16,4]{1,0:T(8,128)S(1)}) custom-call(bf16[1,8,3584]{2,1,0:T(8,128)(2,1)S(1)} %copy-done.2, bf16[1,8,3584]{2,1,0:T(8,128)(2,1)S(1)} %copy-done.3, s32[2,2,1,8,2]{4,3,2,1,0:T(8,128)S(1)} %copy.9.routes, bf16[2,1,3584,4]{3,2,1,0:T(8,128)(2,1)S(1)} %copy.10.router, ...), custom_call_target="tpu_custom_call" | custom-call | tf_op jit(solution)/shard_map/relay/pallas_call | solution.py:350
  118.0 0.7 copy.11
  118.6 0.6 copy.14
  119.2 0.6 copy.15
Async XLA Ops:
  0.6 2.5 %copy-start.3 = (bf16[1,8,3584]{2,1,0:T(8,128)(2,1)S(1)}, bf16[1,8,3584]{2,1,0:T(8,128)(2,1)}, u32[]{:S(2)}) copy-start(bf16[1,8,3584]{2,1,0:T(8,128)(2,1)} %sb.1) | copy-start | bytes 172036
  0.6 2.5 %copy-start.2 = (bf16[1,8,3584]{2,1,0:T(8,128)(2,1)S(1)}, bf16[1,8,3584]{2,1,0:T(8,128)(2,1)}, u32[]{:S(2)}) copy-start(bf16[1,8,3584]{2,1,0:T(8,128)(2,1)} %sa.1) | copy-start | bytes 172036
  3.2 1.5 %copy-start = (bf16[2,1,3584,128]{3,2,1,0:T(8,128)(2,1)S(1)}, bf16[2,1,3584,128]{3,2,1,0:T(8,128)(2,1)}, u32[]{:S(2)}) copy-start(bf16[2,1,3584,128]{3,2,1,0:T(8,128)(2,1)} %up.1) | copy-start | bytes 5505028
  4.7 1.5 %copy-start.1 = (bf16[2,1,128,3584]{3,2,1,0:T(8,128)(2,1)S(1)}, bf16[2,1,128,3584]{3,2,1,0:T(8,128)(2,1)}, u32[]{:S(2)}) copy-start(bf16[2,1,128,3584]{3,2,1,0:T(8,128)(2,1)} %down.1) | copy-start | bytes 5505028

commit v2 on v1

v2 whole, which is shorter than its diff:
```python
import jax
import jax.numpy as jnp
from jax import lax
from jax.experimental import pallas as pl
from jax.experimental.pallas import tpu as pltpu
from jax.sharding import PartitionSpec as P

TICKS = 2
EPS = 1e-06
QUARTERS = 4
CAP = 4
SIDE = 8
SECTIONS = 16
BLOCK = 16
MESH = pl.DeviceIdType.MESH

TO_OWN, TO_OTHER, ON_OWN, ON_OTHER, SWAP_OWN, SWAP_OTHER, HOME, RELAY = range(8)
KINDS = 8


def kernel(
    sa, sb, routes, router, up, down,
    out_a, out_b, out_load,
    u, w, tx, rx, mine, swap_tx, swap_rx, home_tx, home_rx, xtx, xr,
    picks, picks_next, centroids, centroids_next, mtx, mrx,
    send, recv, wlocal, wsend, wrecv, psend, precv, msend, mrecv,
):
    quarter = u.shape[1]
    features = QUARTERS * quarter
    f32, bf16 = jnp.float32, jnp.bfloat16
    pipe = lax.axis_index("pipe")
    ex = lax.axis_index("expert")
    zh = ex // 16
    y = (ex // 2) % SIDE
    core = ex % 2
    turn = 1 - 2 * (y % 2)
    sibling = {"expert": ex + 1 - 2 * core}
    mate = {"expert": ex + 2 * turn}
    ahead = (pipe + 1) % SECTIONS
    behind = (pipe + SECTIONS - 1) % SECTIONS

    def at(plane, to):
        return plane * 16 + to * 2 + core

    targets = [(y + turn * step + SIDE) % SIDE for step in (0, -1, 2, -3)]
    sources = [(y - turn * k + SIDE) % SIDE for k in range(4)]

    px, pz = pipe % 4, pipe // 4
    x_mates = [{"pipe": pz * 4 + (px + k) % 4} for k in range(1, 4)]
    z_mates = [{"pipe": ((pz + k) % 4) * 4 + px} for k in range(1, 4)]
    y_mates = [{"expert": at(zh, (y + k) % SIDE)} for k in range(1, SIDE)]

    def weight_parts(s, which):
        if which == 0:
            return [
                (
                    up.at[s, 0, pl.ds(q * quarter, quarter), :],
                    u.at[s, :, pl.ds(pl.multiple_of(q * 256 + core * 128, 128), 128)],
                )
                for q in range(QUARTERS)
            ]
        return [(down.at[s, 0], w.at[s, pl.ds(pl.multiple_of(core * 128, 128), 128), :])]

    barrier = pltpu.get_barrier_semaphore()

    def greet(device):
        pl.semaphore_signal(barrier, inc=1, device_id=device, device_id_type=MESH)

    greeted = [sibling] + x_mates + z_mates + y_mates
    greeted += [{"expert": at(1 - zh, to)} for to in range(SIDE)]
    for section in (ahead, behind):
        for plane in (zh, 1 - zh):
            greeted += [{"pipe": section, "expert": at(plane, to)} for to in sources]
    for device in greeted:
        greet(device)

    for s in range(2):
        for which in range(2):
            for src, dst in weight_parts(s, which):
                pltpu.make_async_copy(src, dst, wlocal.at[s, which]).start()

    def remote(src, dst, t, s, kind, device):
        return pltpu.make_async_remote_copy(
            src_ref=src, dst_ref=dst, send_sem=send.at[t, s, kind],
            recv_sem=recv.at[t, s, kind], device_id=device, device_id_type=MESH,
        )

    def drain(ref, sem):
        pltpu.make_async_copy(ref, ref, sem).wait()

    def half_of_weight(s, which):
        return u.at[s, :, pl.ds(0, 512)] if which == 0 else w.at[s, pl.ds(0, 128), :]

    def send_weights(s):
        for which in range(2):
            for src, dst in weight_parts(s, which):
                pltpu.make_async_remote_copy(
                    src_ref=src, dst_ref=dst, send_sem=wsend.at[s, which],
                    recv_sem=wrecv.at[s, which], device_id=sibling, device_id_type=MESH,
                ).start()

    def iota(shape, dim):
        return lax.broadcasted_iota(jnp.int32, shape, dim)

    def across(a, b):
        return lax.dot_general(a, b, (((1,), (1,)), ((), ())), preferred_element_type=f32)

    lane4 = iota((8, 4), 1).astype(f32)
    low8 = (iota((8, 8), 0) > iota((8, 8), 1)).astype(bf16)
    eye8 = (iota((8, 8), 0) == iota((8, 8), 1)).astype(bf16)
    expert_hot = (iota((64, 4), 0) // BLOCK == iota((64, 4), 1)).astype(bf16)
    row_t, col_t = iota((64, 32), 0), iota((64, 32), 1)
    same_quarter = (row_t // 4) % 4 == col_t // 8
    slot_t = (row_t % 4).astype(f32)

    for s in range(2):
        for t in range(TICKS):
            picks[t, s, :, 0:2] = across(eye8, routes[t, s, 0].astype(f32).astype(bf16))
        centroids[s] = jnp.concatenate(
            [
                router[s, 0, :, q * quarter : (q + 1) * quarter].astype(f32)
                for q in range(QUARTERS)
            ],
            axis=0,
        ).astype(bf16)

    def send_ahead_of_relay():
        for s, section in ((0, behind), (1, ahead)):
            for i, (src, dst) in enumerate(
                ((picks.at[1, s], picks_next.at[s]), (centroids.at[s], centroids_next.at[s]))
            ):
                pltpu.make_async_remote_copy(
                    src_ref=src, dst_ref=dst, send_sem=psend.at[s, i], recv_sem=precv.at[s, i],
                    device_id={"pipe": section}, device_id_type=MESH,
                ).start()

    def first_rows(s):
        ref = sa if s == 0 else sb
        return [
            ref[0, :, q * quarter : (q + 1) * quarter].astype(f32) for q in range(QUARTERS)
        ]

    def relayed_rows(ref, s):
        rows = ref[s].astype(f32)
        return [rows[q * 8 : (q + 1) * 8] for q in range(QUARTERS)]

    def route(x, picked, central):
        total = sum(jnp.sum(part * part, axis=1, keepdims=True) for part in x)
        scale = lax.rsqrt(total / features + EPS)
        normed4 = jnp.concatenate([part * scale for part in x], axis=0).astype(bf16)
        mixed = across(normed4, central)
        logits = sum(
            mixed[q * 8 : (q + 1) * 8, q * 4 : (q + 1) * 4] for q in range(QUARTERS)
        )
        affinity = jax.nn.sigmoid(logits)
        member = [(picked[:, j : j + 1] == lane4).astype(f32) for j in range(2)]
        chosen = [jnp.sum(m * affinity, axis=1, keepdims=True) for m in member]
        both = chosen[0] + chosen[1]
        gates = (chosen[0] / both) * member[0] + (chosen[1] / both) * member[1]
        selected = member[0] + member[1]
        before = jnp.dot(low8, selected.astype(bf16), preferred_element_type=f32)
        slot = jnp.where(selected > 0, before, -1.0)
        return normed4, gates, slot

    def pack(t, s, normed4, slot):
        slot_of = across(expert_hot, jnp.concatenate([slot] * QUARTERS, axis=0).astype(bf16))
        place = jnp.where(same_quarter & (slot_of == slot_t), 1.0, 0.0).astype(bf16)
        tx[t, s] = jnp.dot(place, normed4, preferred_element_type=f32).astype(bf16)

    def block(index):
        if isinstance(index, int):
            return pl.ds(index * BLOCK, BLOCK)
        return pl.ds(pl.multiple_of(index * BLOCK, BLOCK), BLOCK)

    def blocks(first, count):
        return pl.ds(first * BLOCK, count * BLOCK)

    def dispatch(t, s):
        for plane, kind, base in ((1 - zh, TO_OTHER, 4), (zh, TO_OWN, 0)):
            for k, to in enumerate(targets):
                src = block(plane * 2 + to // 4)
                if t == 0 and base == 0 and k == 0:
                    rx[t, s, block(0)] = tx[t, s, src]
                    continue
                device = {"expert": at(plane, to)}
                if t > 0:
                    device["pipe"] = ahead if s == 0 else behind
                remote(
                    tx.at[t, s, src], rx.at[t, s, block(base + k)], t, s, kind, device
                ).start()

    def pass_on(t, s):
        own = blocks(1, 3) if t == 0 else blocks(0, 4)
        drain(rx.at[t, s, own], recv.at[t, s, TO_OWN])
        remote(rx.at[t, s, blocks(0, 4)], rx.at[t, s, blocks(8, 4)], t, s, ON_OWN, mate).start()
        drain(rx.at[t, s, blocks(4, 4)], recv.at[t, s, TO_OTHER])
        remote(rx.at[t, s, blocks(4, 4)], rx.at[t, s, blocks(12, 4)], t, s, ON_OTHER, mate).start()

    def experts(t, s):
        drain(rx.at[t, s, blocks(8, 4)], recv.at[t, s, ON_OWN])
        drain(rx.at[t, s, blocks(12, 4)], recv.at[t, s, ON_OTHER])
        if t == 0:
            drain(half_of_weight(s, 0), wlocal.at[s, 0])
            drain(half_of_weight(s, 0), wrecv.at[s, 0])
        arrived = rx[t, s]
        lower = iota((16, 8, 256), 1) < 4
        lifted = [
            jnp.dot(
                arrived, u[s, :, q * 256 : (q + 1) * 256], preferred_element_type=f32
            ).reshape(16, 2, 8, 256)
            for q in range(QUARTERS)
        ]
        part = jnp.where(lower, lifted[0][:, 0], lifted[1][:, 0]) + jnp.where(
            lower, lifted[2][:, 1], lifted[3][:, 1]
        )
        part = part.reshape(128, 256)
        lower2 = iota((128, 256), 0) % 8 < 4
        other = jnp.where(lower2, pltpu.roll(part, 124, 0), pltpu.roll(part, 4, 0))
        hidden = jax.nn.silu(part + other).astype(bf16)
        if t == 0:
            drain(half_of_weight(s, 1), wlocal.at[s, 1])
            drain(half_of_weight(s, 1), wrecv.at[s, 1])
        lower3 = iota((128, quarter), 0) % 8 < 4
        halves = []
        for h in range(2):
            two = [
                jnp.dot(
                    hidden, w[s, :, q * quarter : (q + 1) * quarter], preferred_element_type=f32
                )
                for q in (2 * h, 2 * h + 1)
            ]
            halves.append(jnp.where(lower3, two[0], two[1]).reshape(16, 1, 8, quarter))
        both = jnp.concatenate(halves, axis=1).reshape(256, quarter)
        mine[s] = both[0:128]
        swap_tx[t, s] = both[128:256].astype(bf16)
        for kind, first in ((SWAP_OTHER, 4), (SWAP_OWN, 0)):
            remote(
                swap_tx.at[t, s, blocks(first, 4)], swap_rx.at[t, s, blocks(first, 4)],
                t, s, kind, mate,
            ).start()

    def send_home(t, s):
        slot = zh * 4 + y // 2
        for plane, kind, base in ((1 - zh, SWAP_OTHER, 4), (zh, SWAP_OWN, 0)):
            rows = blocks(base, 4)
            drain(swap_rx.at[t, s, rows], recv.at[t, s, kind])
            home_tx[t, s, rows] = (mine[s, rows] + swap_rx[t, s, rows].astype(f32)).astype(bf16)
            for k, to in enumerate(sources):
                if base == 0 and k == 0:
                    home_rx[t, s, block(slot)] = home_tx[t, s, block(0)]
                    continue
                remote(
                    home_tx.at[t, s, block(base + k)], home_rx.at[t, s, block(slot)],
                    t, s, HOME, {"expert": at(plane, to)},
                ).start()

    def finish(t, s, x, gates, slot):
        drain(home_rx.at[t, s, blocks(0, 7)], recv.at[t, s, HOME])
        terms = []
        for e in range(4):
            two = home_rx[t, s, blocks(2 * e, 2)].astype(f32)
            sums = two[0:BLOCK] + two[BLOCK : 2 * BLOCK]
            for c in range(CAP):
                factor = jnp.where(slot[:, e : e + 1] == c, gates[:, e : e + 1], 0.0)
                terms.append((sums, c, factor))
        rows = []
        for q in range(QUARTERS):
            total = x[q]
            for sums, c, factor in terms:
                total = total + factor * sums[q * 4 + c : q * 4 + c + 1, :]
            rows.append(total)
        return rows

    rounds = [[sibling], y_mates, [{"expert": at(1 - zh, y)}], x_mates, z_mates]

    def mass_send(k):
        for i, device in enumerate(rounds[k]):
            pltpu.make_async_remote_copy(
                src_ref=mtx.at[k], dst_ref=mrx.at[k, i], send_sem=msend.at[k],
                recv_sem=mrecv.at[k], device_id=device, device_id_type=MESH,
            ).start()

    def mass_take(k):
        count = len(rounds[k])
        drain(mrx.at[k, pl.ds(0, count)], mrecv.at[k])
        return sum((mrx[k, i] for i in range(count)), mtx[k])

    def mass_step(k):
        mtx[k + 1] = mass_take(k)
        mass_send(k + 1)

    x = [first_rows(s) for s in range(2)]
    routed = [None, None]
    for s in range(2):
        normed4, gates, slot = route(x[s], picks[0, s], centroids[s])
        pack(0, s, normed4, slot)
        routed[s] = (gates, slot)
    pl.semaphore_wait(barrier, len(greeted))
    for s in range(2):
        dispatch(0, s)
    for s in range(2):
        send_weights(s)
    send_ahead_of_relay()
    masses = [jnp.sum(routed[s][0], axis=0, keepdims=True) for s in range(2)]
    for s in range(2):
        pass_on(0, s)
    for s in range(2):
        experts(0, s)
    for s in range(2):
        send_home(0, s)
    for s in range(2):
        rows = finish(0, s, x[s], *routed[s])
        rounded = jnp.concatenate(rows, axis=0).astype(bf16)
        xtx[s] = rounded
        if s == 0:
            for i in range(2):
                for j in range(2):
                    ref = (picks_next if j == 0 else centroids_next).at[i]
                    drain(ref, precv.at[i, j])
        normed4, _, slot = route(relayed_rows(xtx, s), picks_next[s], centroids_next[s])
        pack(1, s, normed4, slot)
        dispatch(1, s)
        remote(
            xtx.at[s], xr.at[s], 0, s, RELAY, {"pipe": ahead if s == 0 else behind}
        ).start()

    for s in range(2):
        pass_on(1, s)
    for s in range(2):
        drain(xr.at[s], recv.at[0, s, RELAY])
        x[s] = relayed_rows(xr, s)
        _, gates, slot = route(x[s], picks[1, s], centroids[s])
        routed[s] = (gates, slot)
        masses[s] = masses[s] + jnp.sum(gates, axis=0, keepdims=True)
    row = iota((16, 4), 0)
    mtx[0] = jnp.zeros_like(mtx[0])
    mtx[0, :, 0:4] = jnp.where(row == pipe, masses[0], 0.0) + jnp.where(
        row == SECTIONS - 1 - pipe, masses[1], 0.0
    )
    mass_send(0)
    for s in range(2):
        experts(1, s)
        mass_step(s)
    for s in range(2):
        send_home(1, s)
        mass_step(2 + s)
    for s in range(2):
        rows = finish(1, s, x[s], *routed[s])
        ref = out_a if s == 0 else out_b
        for q in range(QUARTERS):
            ref[0, :, q * quarter : (q + 1) * quarter] = rows[q].astype(bf16)
    out_load[...] = mass_take(4)[:, 0:4] / (2 * TICKS * 8 * 32)

    for s in range(2):
        for which in range(2):
            drain(half_of_weight(s, which), wsend.at[s, which])
        drain(picks_next.at[s], psend.at[s, 0])
        drain(centroids_next.at[s], psend.at[s, 1])
    for k in range(5):
        drain(mrx.at[k, pl.ds(0, len(rounds[k]))], msend.at[k])
    for s in range(2):
        drain(xr.at[s], send.at[0, s, RELAY])
        for t in range(TICKS):
            drain(rx.at[t, s, blocks(0, 3 + t)], send.at[t, s, TO_OWN])
            for kind in (TO_OTHER, ON_OWN, ON_OTHER, SWAP_OWN, SWAP_OTHER):
                drain(rx.at[t, s, blocks(0, 4)], send.at[t, s, kind])
            drain(home_rx.at[t, s, blocks(0, 7)], send.at[t, s, HOME])


def shards(stream_a, stream_b, routes, up_weight, down_weight, router_weight):
    features = stream_a.shape[2]
    quarter = features // QUARTERS
    vmem = pl.BlockSpec(memory_space=pltpu.VMEM)
    hbm = pl.BlockSpec(memory_space=pl.ANY)
    bf16, f32 = jnp.bfloat16, jnp.float32
    return pl.pallas_call(
        kernel,
        out_shape=(
            jax.ShapeDtypeStruct(stream_a.shape, bf16),
            jax.ShapeDtypeStruct(stream_b.shape, bf16),
            jax.ShapeDtypeStruct((16, 4), f32),
        ),
        in_specs=[vmem, vmem, vmem, vmem, hbm, hbm],
        out_specs=(vmem, vmem, vmem),
        scratch_shapes=[
            pltpu.VMEM((2, quarter, QUARTERS * 256), bf16),
            pltpu.VMEM((2, 256, features), bf16),
            pltpu.VMEM((TICKS, 2, 64, quarter), bf16),
            pltpu.VMEM((TICKS, 2, 256, quarter), bf16),
            pltpu.VMEM((2, 128, quarter), f32),
            pltpu.VMEM((TICKS, 2, 128, quarter), bf16),
            pltpu.VMEM((TICKS, 2, 128, quarter), bf16),
            pltpu.VMEM((TICKS, 2, 128, quarter), bf16),
            pltpu.VMEM((TICKS, 2, 128, quarter), bf16),
            pltpu.VMEM((2, 32, quarter), bf16),
            pltpu.VMEM((2, 32, quarter), bf16),
            pltpu.VMEM((TICKS, 2, 8, 128), f32),
            pltpu.VMEM((2, 8, 128), f32),
            pltpu.VMEM((2, 16, quarter), bf16),
            pltpu.VMEM((2, 16, quarter), bf16),
            pltpu.VMEM((5, 16, 128), f32),
            pltpu.VMEM((5, SIDE - 1, 16, 128), f32),
            pltpu.SemaphoreType.DMA((TICKS, 2, KINDS)),
            pltpu.SemaphoreType.DMA((TICKS, 2, KINDS)),
            pltpu.SemaphoreType.DMA((2, 2)),
            pltpu.SemaphoreType.DMA((2, 2)),
            pltpu.SemaphoreType.DMA((2, 2)),
            pltpu.SemaphoreType.DMA((2, 2)),
            pltpu.SemaphoreType.DMA((2, 2)),
            pltpu.SemaphoreType.DMA((5,)),
            pltpu.SemaphoreType.DMA((5,)),
        ],
        compiler_params=pltpu.CompilerParams(
            collective_id=0, has_side_effects=True, vmem_limit_bytes=60 * 2**20
        ),
        name="relay",
    )(
        stream_a, stream_b, jnp.swapaxes(routes, 3, 4), jnp.swapaxes(router_weight, 2, 3),
        up_weight, down_weight,
    )


def solution(mesh):
    return jax.shard_map(
        shards,
        mesh=mesh,
        in_specs=(
            P("pipe", "expert", None),
            P("pipe", "expert", None),
            P(None, None, "pipe", "expert", None),
            P(None, "pipe", None, "expert"),
            P(None, "pipe", "expert", None),
            P(None, "pipe", None, None),
        ),
        out_specs=(P("pipe", "expert", None), P("pipe", "expert", None), P()),
        check_vma=False,
    )
```

time: 120 us -> 107 us (0.89)
  the two profiles are of different devices: /device:TPU:8 before, /device:TPU:4 now
where the time goes in v2:
time: 107 us
  Pallas kernels  102 us (95%)
  local copies, waits for them, and re-layouts  4.24 us (4%)
    pallas_call x1, Pallas kernels, shards(): pl.pallas_call(kernel, out_shape=(jax.ShapeDtypeStruct(stream_a.shape, bf...  102 us
    unnamed x2, local copies, waits for them, and re-layouts  2.89 us

profile of v2, /device:TPU:4, one launch (start us, length us, event | category | flops | bytes accessed | tf_op | source)
XLA Modules:
  0.0 107.0 jit_solution(16920866913245743446)
XLA Ops:
  0.6 102.1 %relay.1 = (bf16[1,8,3584]{2,1,0:T(8,128)(2,1)}, bf16[1,8,3584]{2,1,0:T(8,128)(2,1)}, f32[16,4]{1,0:T(8,128)}) custom-call(bf16[1,8,3584]{2,1,0:T(8,128)(2,1)} %sa.1, bf16[1,8,3584]{2,1,0:T(8,128)(2,1)} %sb.1, s32[2,2,1,2,8]{4,3,2,1,0:T(2,128)} %bitcast.3, bf16[2,1,4,3584]{3,2,1,0:T(4,128)(2,1)} %bitcast.2, bf16[2,1,3584,128]{3,2,1,0:T(8,128)(2,1)} %up.1, ...), custom_call_target="tpu_custom_call" | custom-call | tf_op jit(solution)/shard_map/relay/pallas_call | solution.py:376
  102.7 1.3 %copy.9 = f32[16,4]{0,1:T(4,128)} copy(f32[16,4]{1,0:T(8,128)} %get-tuple-element.5) | data formatting | bytes 512 | tf_op jit(solution)/shard_map/relay/pallas_call | solution.py:376
  104.1 1.4 %copy.12 = bf16[1,8,3584]{2,1,0:T(8,128)(2,1)} copy(bf16[1,8,3584]{2,1,0:T(8,128)(2,1)} %get-tuple-element.9) | data formatting | bytes 114688
  105.5 1.4 %copy.13 = bf16[1,8,3584]{2,1,0:T(8,128)(2,1)} copy(bf16[1,8,3584]{2,1,0:T(8,128)(2,1)} %get-tuple-element.10) | data formatting | bytes 114688

commit v3 on v2

--- a/solution.py
+++ b/solution.py
@@ -19,11 +19,11 @@
 
 
 def kernel(
-    sa, sb, routes, router, up, down,
+    sa, sb, routes_in, router_in, up, down,
     out_a, out_b, out_load,
-    u, w, tx, rx, mine, swap_tx, swap_rx, home_tx, home_rx, xtx, xr,
+    xin, routes, router, u, w, tx, rx, mine, swap_tx, swap_rx, home_tx, home_rx, xtx, xr,
     picks, picks_next, centroids, centroids_next, mtx, mrx,
-    send, recv, wlocal, wsend, wrecv, psend, precv, msend, mrecv,
+    send, recv, inputs, wlocal, wsend, wrecv, psend, precv, msend, mrecv,
 ):
     quarter = u.shape[1]
     features = QUARTERS * quarter
@@ -48,7 +48,6 @@
     px, pz = pipe % 4, pipe // 4
     x_mates = [{"pipe": pz * 4 + (px + k) % 4} for k in range(1, 4)]
     z_mates = [{"pipe": ((pz + k) % 4) * 4 + px} for k in range(1, 4)]
-    y_mates = [{"expert": at(zh, (y + k) % SIDE)} for k in range(1, SIDE)]
 
     def weight_parts(s, which):
         if which == 0:
@@ -66,14 +65,28 @@
     def greet(device):
         pl.semaphore_signal(barrier, inc=1, device_id=device, device_id_type=MESH)
 
-    greeted = [sibling] + x_mates + z_mates + y_mates
-    greeted += [{"expert": at(1 - zh, to)} for to in range(SIDE)]
-    for section in (ahead, behind):
-        for plane in (zh, 1 - zh):
-            greeted += [{"pipe": section, "expert": at(plane, to)} for to in sources]
+    near = [(y + step + SIDE) % SIDE for step in (2, -2)] + [
+        (y + turn * step + SIDE) % SIDE for step in (-1, -3)
+    ]
+    greeted = [{"expert": at(1 - zh, to)} for to in near + [y]]
+    greeted += [{"expert": at(zh, to)} for to in near] + [{"pipe": ahead}, {"pipe": behind}]
+    greeted += x_mates + z_mates + [mate, sibling]
     for device in greeted:
         greet(device)
 
+    input_copies = [
+        pltpu.make_async_copy(src, dst, inputs.at[i])
+        for i, (src, dst) in enumerate(
+            (
+                (sa.at[0], xin.at[0]),
+                (sb.at[0], xin.at[1]),
+                (routes_in, routes),
+                (router_in, router),
+            )
+        )
+    ]
+    for copy in input_copies:
+        copy.start()
     for s in range(2):
         for which in range(2):
             for src, dst in weight_parts(s, which):
@@ -112,6 +125,9 @@
     row_t, col_t = iota((64, 32), 0), iota((64, 32), 1)
     same_quarter = (row_t // 4) % 4 == col_t // 8
     slot_t = (row_t % 4).astype(f32)
+
+    for copy in input_copies:
+        copy.wait()
 
     for s in range(2):
         for t in range(TICKS):
@@ -135,9 +151,8 @@
                 ).start()
 
     def first_rows(s):
-        ref = sa if s == 0 else sb
         return [
-            ref[0, :, q * quarter : (q + 1) * quarter].astype(f32) for q in range(QUARTERS)
+            xin[s, :, q * quarter : (q + 1) * quarter].astype(f32) for q in range(QUARTERS)
         ]
 
     def relayed_rows(ref, s):
@@ -176,8 +191,8 @@
         return pl.ds(first * BLOCK, count * BLOCK)
 
     def dispatch(t, s):
-        for plane, kind, base in ((1 - zh, TO_OTHER, 4), (zh, TO_OWN, 0)):
-            for k, to in enumerate(targets):
+        for plane, kind, base in ((zh, TO_OWN, 0), (1 - zh, TO_OTHER, 4)):
+            for k, to in reversed(list(enumerate(targets))):
                 src = block(plane * 2 + to // 4)
                 if t == 0 and base == 0 and k == 0:
                     rx[t, s, block(0)] = tx[t, s, src]
@@ -189,12 +204,18 @@
                     tx.at[t, s, src], rx.at[t, s, block(base + k)], t, s, kind, device
                 ).start()
 
-    def pass_on(t, s):
+    def pass_on(t, s, group=None):
+        if group is None:
+            pass_on(t, s, 0)
+            pass_on(t, s, 1)
+            return
         own = blocks(1, 3) if t == 0 else blocks(0, 4)
+        if group == 1:
+            drain(rx.at[t, s, blocks(4, 4)], recv.at[t, s, TO_OTHER])
+            remote(rx.at[t, s, blocks(4, 4)], rx.at[t, s, blocks(12, 4)], t, s, ON_OTHER, mate).start()
+            return
         drain(rx.at[t, s, own], recv.at[t, s, TO_OWN])
         remote(rx.at[t, s, blocks(0, 4)], rx.at[t, s, blocks(8, 4)], t, s, ON_OWN, mate).start()
-        drain(rx.at[t, s, blocks(4, 4)], recv.at[t, s, TO_OTHER])
-        remote(rx.at[t, s, blocks(4, 4)], rx.at[t, s, blocks(12, 4)], t, s, ON_OTHER, mate).start()
 
     def experts(t, s):
         drain(rx.at[t, s, blocks(8, 4)], recv.at[t, s, ON_OWN])
@@ -245,7 +266,7 @@
             rows = blocks(base, 4)
             drain(swap_rx.at[t, s, rows], recv.at[t, s, kind])
             home_tx[t, s, rows] = (mine[s, rows] + swap_rx[t, s, rows].astype(f32)).astype(bf16)
-            for k, to in enumerate(sources):
+            for k, to in reversed(list(enumerate(sources))):
                 if base == 0 and k == 0:
                     home_rx[t, s, block(slot)] = home_tx[t, s, block(0)]
                     continue
@@ -271,7 +292,9 @@
             rows.append(total)
         return rows
 
-    rounds = [[sibling], y_mates, [{"expert": at(1 - zh, y)}], x_mates, z_mates]
+    spread = [{"expert": at(zh, to)} for to in targets[1:]]
+    spread += [{"expert": at(1 - zh, to)} for to in targets]
+    rounds = [[sibling], spread, [mate], x_mates, z_mates]
 
     def mass_send(k):
         for i, device in enumerate(rounds[k]):
@@ -301,49 +324,53 @@
     for s in range(2):
         send_weights(s)
     send_ahead_of_relay()
-    masses = [jnp.sum(routed[s][0], axis=0, keepdims=True) for s in range(2)]
-    for s in range(2):
-        pass_on(0, s)
+    row = iota((16, 4), 0)
+
+    def mass_rows(gates, layer):
+        return jnp.where(row == layer, jnp.sum(gates, axis=0, keepdims=True), 0.0)
+
+    masses = mass_rows(routed[0][0], pipe) + mass_rows(routed[1][0], SECTIONS - 1 - pipe)
+    for g in range(2):
+        for s in range(2):
+            pass_on(0, s, g)
     for s in range(2):
         experts(0, s)
     for s in range(2):
         send_home(0, s)
+    for i in range(2):
+        drain(picks_next.at[i], precv.at[i, 0])
+        drain(centroids_next.at[i], precv.at[i, 1])
     for s in range(2):
         rows = finish(0, s, x[s], *routed[s])
-        rounded = jnp.concatenate(rows, axis=0).astype(bf16)
-        xtx[s] = rounded
-        if s == 0:
-            for i in range(2):
-                for j in range(2):
-                    ref = (picks_next if j == 0 else centroids_next).at[i]
-                    drain(ref, precv.at[i, j])
-        normed4, _, slot = route(relayed_rows(xtx, s), picks_next[s], centroids_next[s])
+        xtx[s] = jnp.concatenate(rows, axis=0).astype(bf16)
+        normed4, gates, slot = route(relayed_rows(xtx, s), picks_next[s], centroids_next[s])
         pack(1, s, normed4, slot)
         dispatch(1, s)
         remote(
             xtx.at[s], xr.at[s], 0, s, RELAY, {"pipe": ahead if s == 0 else behind}
         ).start()
-
-    for s in range(2):
-        pass_on(1, s)
+        masses = masses + mass_rows(gates, ahead if s == 0 else SECTIONS - 1 - behind)
+    mtx[0] = jnp.zeros_like(mtx[0])
+    mtx[0, :, 0:4] = masses
+    mass_send(0)
+
+    pass_on(1, 0, 0)
+    mass_step(0)
+    pass_on(1, 1, 0)
+    pass_on(1, 0, 1)
+    pass_on(1, 1, 1)
     for s in range(2):
         drain(xr.at[s], recv.at[0, s, RELAY])
         x[s] = relayed_rows(xr, s)
         _, gates, slot = route(x[s], picks[1, s], centroids[s])
         routed[s] = (gates, slot)
-        masses[s] = masses[s] + jnp.sum(gates, axis=0, keepdims=True)
-    row = iota((16, 4), 0)
-    mtx[0] = jnp.zeros_like(mtx[0])
-    mtx[0, :, 0:4] = jnp.where(row == pipe, masses[0], 0.0) + jnp.where(
-        row == SECTIONS - 1 - pipe, masses[1], 0.0
-    )
-    mass_send(0)
-    for s in range(2):
-        experts(1, s)
-        mass_step(s)
-    for s in range(2):
-        send_home(1, s)
-        mass_step(2 + s)
+    experts(1, 0)
+    mass_step(1)
+    experts(1, 1)
+    mass_step(2)
+    send_home(1, 0)
+    send_home(1, 1)
+    mass_step(3)
     for s in range(2):
         rows = finish(1, s, x[s], *routed[s])
         ref = out_a if s == 0 else out_b
@@ -367,22 +394,31 @@
             drain(home_rx.at[t, s, blocks(0, 7)], send.at[t, s, HOME])
 
 
+def hand_over(a, b, load, out_a, out_b, out_load):
+    out_a[...] = a[...]
+    out_b[...] = b[...]
+    out_load[...] = load[...].T
+
+
 def shards(stream_a, stream_b, routes, up_weight, down_weight, router_weight):
     features = stream_a.shape[2]
     quarter = features // QUARTERS
     vmem = pl.BlockSpec(memory_space=pltpu.VMEM)
-    hbm = pl.BlockSpec(memory_space=pl.ANY)
+    hbm = pl.BlockSpec(memory_space=pltpu.HBM)
     bf16, f32 = jnp.bfloat16, jnp.float32
-    return pl.pallas_call(
+    results = pl.pallas_call(
         kernel,
         out_shape=(
             jax.ShapeDtypeStruct(stream_a.shape, bf16),
             jax.ShapeDtypeStruct(stream_b.shape, bf16),
             jax.ShapeDtypeStruct((16, 4), f32),
         ),
-        in_specs=[vmem, vmem, vmem, vmem, hbm, hbm],
+        in_specs=[hbm] * 6,
         out_specs=(vmem, vmem, vmem),
         scratch_shapes=[
+            pltpu.VMEM((2, 8, features), bf16),
+            pltpu.VMEM((TICKS, 2, 1, 2, 8), jnp.int32),
+            pltpu.VMEM((2, 1, 4, features), bf16),
             pltpu.VMEM((2, quarter, QUARTERS * 256), bf16),
             pltpu.VMEM((2, 256, features), bf16),
             pltpu.VMEM((TICKS, 2, 64, quarter), bf16),
@@ -402,6 +438,7 @@
             pltpu.VMEM((5, SIDE - 1, 16, 128), f32),
             pltpu.SemaphoreType.DMA((TICKS, 2, KINDS)),
             pltpu.SemaphoreType.DMA((TICKS, 2, KINDS)),
+            pltpu.SemaphoreType.DMA((4,)),
             pltpu.SemaphoreType.DMA((2, 2)),
             pltpu.SemaphoreType.DMA((2, 2)),
             pltpu.SemaphoreType.DMA((2, 2)),
@@ -411,13 +448,26 @@
             pltpu.SemaphoreType.DMA((5,)),
         ],
         compiler_params=pltpu.CompilerParams(
-            collective_id=0, has_side_effects=True, vmem_limit_bytes=60 * 2**20
+            collective_id=0, has_side_effects=True, vmem_limit_bytes=55 * 2**20
         ),
         name="relay",
     )(
         stream_a, stream_b, jnp.swapaxes(routes, 3, 4), jnp.swapaxes(router_weight, 2, 3),
         up_weight, down_weight,
     )
+    final_a, final_b, load = pl.pallas_call(
+        hand_over,
+        out_shape=(
+            jax.ShapeDtypeStruct(stream_a.shape, bf16),
+            jax.ShapeDtypeStruct(stream_b.shape, bf16),
+            jax.ShapeDtypeStruct((4, 16), f32),
+        ),
+        in_specs=[vmem] * 3,
+        out_specs=(vmem,) * 3,
+        compiler_params=pltpu.CompilerParams(vmem_limit_bytes=55 * 2**20),
+        name="hand_over",
+    )(*results)
+    return final_a, final_b, load.T
 
 
 def solution(mesh):

time: 107 us -> 95.5 us (0.89)
  the two profiles are of different devices: /device:TPU:4 before, /device:TPU:24 now
where the time goes in v3:
time: 95.5 us; the launch traced here: 95.3 us
  Pallas kernels  94.6 us (99%)
    pallas_call x1, Pallas kernels, shards(): pl.pallas_call(kernel, out_shape=(jax.ShapeDtypeStruct(stream_a.shape, bf...  93.1 us

profile of v3, /device:TPU:24, one launch (start us, length us, event | category | flops | bytes accessed | tf_op | source)
XLA Modules:
  0.0 95.3 jit_solution(2173777020670661076)
XLA Ops:
  0.6 93.1 %relay.1 = (bf16[1,8,3584]{2,1,0:T(8,128)(2,1)}, bf16[1,8,3584]{2,1,0:T(8,128)(2,1)}, f32[16,4]{1,0:T(8,128)}) custom-call(bf16[1,8,3584]{2,1,0:T(8,128)(2,1)} %sa.1, bf16[1,8,3584]{2,1,0:T(8,128)(2,1)} %sb.1, s32[2,2,1,2,8]{4,3,2,1,0:T(2,128)} %bitcast.4, bf16[2,1,4,3584]{3,2,1,0:T(4,128)(2,1)} %bitcast.3, bf16[2,1,3584,128]{3,2,1,0:T(8,128)(2,1)} %up.1, ...), custom_call_target="tpu_custom_call" | custom-call | tf_op jit(solution)/shard_map/relay/pallas_call | solution.py:409
  93.8 1.5 %hand_over.1 = (bf16[1,8,3584]{2,1,0:T(8,128)(2,1)}, bf16[1,8,3584]{2,1,0:T(8,128)(2,1)}, f32[4,16]{1,0:T(4,128)}) custom-call(bf16[1,8,3584]{2,1,0:T(8,128)(2,1)} %get-tuple-element.9.a, bf16[1,8,3584]{2,1,0:T(8,128)(2,1)} %get-tuple-element.10.b, f32[16,4]{1,0:T(8,128)} %get-tuple-element.11.load), custom_call_target="tpu_custom_call" | custom-call | tf_op jit(solution)/shard_map/hand_over/pallas_call | solution.py:458

commit v4 on v3

--- a/solution.py
+++ b/solution.py
@@ -15,7 +15,8 @@
 MESH = pl.DeviceIdType.MESH
 
 TO_OWN, TO_OTHER, ON_OWN, ON_OTHER, SWAP_OWN, SWAP_OTHER, HOME, RELAY = range(8)
-KINDS = 8
+TO_OTHER_FAR = 8
+KINDS = 9
 
 
 def kernel(
@@ -104,13 +105,12 @@
     def half_of_weight(s, which):
         return u.at[s, :, pl.ds(0, 512)] if which == 0 else w.at[s, pl.ds(0, 128), :]
 
-    def send_weights(s):
-        for which in range(2):
-            for src, dst in weight_parts(s, which):
-                pltpu.make_async_remote_copy(
-                    src_ref=src, dst_ref=dst, send_sem=wsend.at[s, which],
-                    recv_sem=wrecv.at[s, which], device_id=sibling, device_id_type=MESH,
-                ).start()
+    def send_weights(s, which):
+        for src, dst in weight_parts(s, which):
+            pltpu.make_async_remote_copy(
+                src_ref=src, dst_ref=dst, send_sem=wsend.at[s, which],
+                recv_sem=wrecv.at[s, which], device_id=sibling, device_id_type=MESH,
+            ).start()
 
     def iota(shape, dim):
         return lax.broadcasted_iota(jnp.int32, shape, dim)
@@ -159,27 +159,33 @@
         rows = ref[s].astype(f32)
         return [rows[q * 8 : (q + 1) * 8] for q in range(QUARTERS)]
 
-    def route(x, picked, central):
+    def seats(picked):
+        member = [(picked[:, j : j + 1] == lane4).astype(f32) for j in range(2)]
+        selected = member[0] + member[1]
+        before = jnp.dot(low8, selected.astype(bf16), preferred_element_type=f32)
+        slot = jnp.where(selected > 0, before, -1.0)
+        return member, slot
+
+    def placing(slot):
+        slot_of = across(expert_hot, jnp.concatenate([slot] * QUARTERS, axis=0).astype(bf16))
+        return jnp.where(same_quarter & (slot_of == slot_t), 1.0, 0.0).astype(bf16)
+
+    def normalize(x):
         total = sum(jnp.sum(part * part, axis=1, keepdims=True) for part in x)
         scale = lax.rsqrt(total / features + EPS)
-        normed4 = jnp.concatenate([part * scale for part in x], axis=0).astype(bf16)
+        return jnp.concatenate([part * scale for part in x], axis=0).astype(bf16)
+
+    def gating(normed4, member, central):
         mixed = across(normed4, central)
         logits = sum(
             mixed[q * 8 : (q + 1) * 8, q * 4 : (q + 1) * 4] for q in range(QUARTERS)
         )
         affinity = jax.nn.sigmoid(logits)
-        member = [(picked[:, j : j + 1] == lane4).astype(f32) for j in range(2)]
         chosen = [jnp.sum(m * affinity, axis=1, keepdims=True) for m in member]
         both = chosen[0] + chosen[1]
-        gates = (chosen[0] / both) * member[0] + (chosen[1] / both) * member[1]
-        selected = member[0] + member[1]
-        before = jnp.dot(low8, selected.astype(bf16), preferred_element_type=f32)
-        slot = jnp.where(selected > 0, before, -1.0)
-        return normed4, gates, slot
-
-    def pack(t, s, normed4, slot):
-        slot_of = across(expert_hot, jnp.concatenate([slot] * QUARTERS, axis=0).astype(bf16))
-        place = jnp.where(same_quarter & (slot_of == slot_t), 1.0, 0.0).astype(bf16)
+        return (chosen[0] / both) * member[0] + (chosen[1] / both) * member[1]
+
+    def pack(t, s, normed4, place):
         tx[t, s] = jnp.dot(place, normed4, preferred_element_type=f32).astype(bf16)
 
     def block(index):
@@ -200,22 +206,26 @@
                 device = {"expert": at(plane, to)}
                 if t > 0:
                     device["pipe"] = ahead if s == 0 else behind
+                by = TO_OTHER_FAR if base == 4 and k > 1 else kind
                 remote(
-                    tx.at[t, s, src], rx.at[t, s, block(base + k)], t, s, kind, device
+                    tx.at[t, s, src], rx.at[t, s, block(base + k)], t, s, by, device
                 ).start()
 
-    def pass_on(t, s, group=None):
-        if group is None:
-            pass_on(t, s, 0)
-            pass_on(t, s, 1)
+    def pass_on(t, s, group):
+        if group == 1:
+            for kind, first in ((TO_OTHER_FAR, 6), (TO_OTHER, 4)):
+                drain(rx.at[t, s, blocks(first, 2)], recv.at[t, s, kind])
+                remote(
+                    rx.at[t, s, blocks(first, 2)], rx.at[t, s, blocks(8 + first, 2)],
+                    t, s, ON_OTHER, mate,
+                ).start()
             return
-        own = blocks(1, 3) if t == 0 else blocks(0, 4)
-        if group == 1:
-            drain(rx.at[t, s, blocks(4, 4)], recv.at[t, s, TO_OTHER])
-            remote(rx.at[t, s, blocks(4, 4)], rx.at[t, s, blocks(12, 4)], t, s, ON_OTHER, mate).start()
-            return
-        drain(rx.at[t, s, own], recv.at[t, s, TO_OWN])
-        remote(rx.at[t, s, blocks(0, 4)], rx.at[t, s, blocks(8, 4)], t, s, ON_OWN, mate).start()
+        got = blocks(1, 3) if t == 0 else blocks(0, 4)
+        drain(rx.at[t, s, got], recv.at[t, s, TO_OWN + group])
+        remote(
+            rx.at[t, s, blocks(group * 4, 4)], rx.at[t, s, blocks(8 + group * 4, 4)],
+            t, s, ON_OWN + group, mate,
+        ).start()
 
     def experts(t, s):
         drain(rx.at[t, s, blocks(8, 4)], recv.at[t, s, ON_OWN])
@@ -254,26 +264,28 @@
         both = jnp.concatenate(halves, axis=1).reshape(256, quarter)
         mine[s] = both[0:128]
         swap_tx[t, s] = both[128:256].astype(bf16)
-        for kind, first in ((SWAP_OTHER, 4), (SWAP_OWN, 0)):
+        swap(t, s, 1)
+
+    def swap(t, s, group):
+        rows = blocks(group * 4, 4)
+        remote(
+            swap_tx.at[t, s, rows], swap_rx.at[t, s, rows], t, s, SWAP_OWN + group, mate
+        ).start()
+
+    def send_home(t, s, group):
+        slot = zh * 4 + y // 2
+        plane = 1 - zh if group else zh
+        rows = blocks(group * 4, 4)
+        drain(swap_rx.at[t, s, rows], recv.at[t, s, SWAP_OWN + group])
+        home_tx[t, s, rows] = (mine[s, rows] + swap_rx[t, s, rows].astype(f32)).astype(bf16)
+        for k, to in reversed(list(enumerate(sources))):
+            if group == 0 and k == 0:
+                home_rx[t, s, block(slot)] = home_tx[t, s, block(0)]
+                continue
             remote(
-                swap_tx.at[t, s, blocks(first, 4)], swap_rx.at[t, s, blocks(first, 4)],
-                t, s, kind, mate,
+                home_tx.at[t, s, block(group * 4 + k)], home_rx.at[t, s, block(slot)],
+                t, s, HOME, {"expert": at(plane, to)},
             ).start()
-
-    def send_home(t, s):
-        slot = zh * 4 + y // 2
-        for plane, kind, base in ((1 - zh, SWAP_OTHER, 4), (zh, SWAP_OWN, 0)):
-            rows = blocks(base, 4)
-            drain(swap_rx.at[t, s, rows], recv.at[t, s, kind])
-            home_tx[t, s, rows] = (mine[s, rows] + swap_rx[t, s, rows].astype(f32)).astype(bf16)
-            for k, to in reversed(list(enumerate(sources))):
-                if base == 0 and k == 0:
-                    home_rx[t, s, block(slot)] = home_tx[t, s, block(0)]
-                    continue
-                remote(
-                    home_tx.at[t, s, block(base + k)], home_rx.at[t, s, block(slot)],
-                    t, s, HOME, {"expert": at(plane, to)},
-                ).start()
 
     def finish(t, s, x, gates, slot):
         drain(home_rx.at[t, s, blocks(0, 7)], recv.at[t, s, HOME])
@@ -314,68 +326,105 @@
 
     x = [first_rows(s) for s in range(2)]
     routed = [None, None]
+    seated = [[seats(picks[t, s]) for s in range(2)] for t in range(TICKS)]
     for s in range(2):
-        normed4, gates, slot = route(x[s], picks[0, s], centroids[s])
-        pack(0, s, normed4, slot)
-        routed[s] = (gates, slot)
+        normed4 = normalize(x[s])
+        member, slot = seated[0][s]
+        pack(0, s, normed4, placing(slot))
+        routed[s] = (gating(normed4, member, centroids[s]), slot)
     pl.semaphore_wait(barrier, len(greeted))
-    for s in range(2):
-        dispatch(0, s)
-    for s in range(2):
-        send_weights(s)
-    send_ahead_of_relay()
     row = iota((16, 4), 0)
 
     def mass_rows(gates, layer):
         return jnp.where(row == layer, jnp.sum(gates, axis=0, keepdims=True), 0.0)
 
-    masses = mass_rows(routed[0][0], pipe) + mass_rows(routed[1][0], SECTIONS - 1 - pipe)
-    for g in range(2):
-        for s in range(2):
-            pass_on(0, s, g)
-    for s in range(2):
-        experts(0, s)
-    for s in range(2):
-        send_home(0, s)
-    for i in range(2):
-        drain(picks_next.at[i], precv.at[i, 0])
-        drain(centroids_next.at[i], precv.at[i, 1])
-    for s in range(2):
-        rows = finish(0, s, x[s], *routed[s])
-        xtx[s] = jnp.concatenate(rows, axis=0).astype(bf16)
-        normed4, gates, slot = route(relayed_rows(xtx, s), picks_next[s], centroids_next[s])
-        pack(1, s, normed4, slot)
+    masses = [mass_rows(routed[0][0], pipe) + mass_rows(routed[1][0], SECTIONS - 1 - pipe)]
+
+    def first(s):
+        dispatch(0, s)
+        if s == 1:
+            send_ahead_of_relay()
+
+    next_seats = [None, None]
+
+    def look_ahead(s):
+        drain(picks_next.at[s], precv.at[s, 0])
+        drain(centroids_next.at[s], precv.at[s, 1])
+        member, slot = seats(picks_next[s])
+        next_seats[s] = (member, placing(slot))
+
+    def between(s):
+        xtx[s] = jnp.concatenate(finish(0, s, x[s], *routed[s]), axis=0).astype(bf16)
+        normed4 = normalize(relayed_rows(xtx, s))
+        member, place = next_seats[s]
+        pack(1, s, normed4, place)
         dispatch(1, s)
         remote(
             xtx.at[s], xr.at[s], 0, s, RELAY, {"pipe": ahead if s == 0 else behind}
         ).start()
-        masses = masses + mass_rows(gates, ahead if s == 0 else SECTIONS - 1 - behind)
-    mtx[0] = jnp.zeros_like(mtx[0])
-    mtx[0, :, 0:4] = masses
-    mass_send(0)
-
+        gates = gating(normed4, member, centroids_next[s])
+        masses.append(mass_rows(gates, ahead if s == 0 else SECTIONS - 1 - behind))
+
+    def mass_start():
+        mtx[0] = jnp.zeros_like(mtx[0])
+        mtx[0, :, 0:4] = sum(masses)
+        mass_send(0)
+
+    def again(s):
+        drain(xr.at[s], recv.at[0, s, RELAY])
+        x[s] = relayed_rows(xr, s)
+        member, slot = seated[1][s]
+        routed[s] = (gating(normalize(x[s]), member, centroids[s]), slot)
+
+    def last(s):
+        rows = finish(1, s, x[s], *routed[s])
+        ref = out_a if s == 0 else out_b
+        for q in range(QUARTERS):
+            ref[0, :, q * quarter : (q + 1) * quarter] = rows[q].astype(bf16)
+
+    first(0)
+    first(1)
+    send_weights(0, 0)
+    send_weights(0, 1)
+    send_weights(1, 0)
+    send_weights(1, 1)
+    pass_on(0, 0, 0)
+    pass_on(0, 1, 0)
+    pass_on(0, 0, 1)
+    pass_on(0, 1, 1)
+    experts(0, 0)
+    experts(0, 1)
+    swap(0, 0, 0)
+    swap(0, 1, 0)
+    look_ahead(0)
+    look_ahead(1)
+    send_home(0, 0, 1)
+    send_home(0, 1, 1)
+    send_home(0, 0, 0)
+    send_home(0, 1, 0)
+    between(0)
+    between(1)
+    mass_start()
     pass_on(1, 0, 0)
     mass_step(0)
     pass_on(1, 1, 0)
     pass_on(1, 0, 1)
     pass_on(1, 1, 1)
-    for s in range(2):
-        drain(xr.at[s], recv.at[0, s, RELAY])
-        x[s] = relayed_rows(xr, s)
-        _, gates, slot = route(x[s], picks[1, s], centroids[s])
-        routed[s] = (gates, slot)
+    again(0)
+    again(1)
     experts(1, 0)
     mass_step(1)
     experts(1, 1)
+    swap(1, 0, 0)
+    swap(1, 1, 0)
     mass_step(2)
-    send_home(1, 0)
-    send_home(1, 1)
+    send_home(1, 0, 1)
+    send_home(1, 1, 1)
+    send_home(1, 0, 0)
+    send_home(1, 1, 0)
     mass_step(3)
-    for s in range(2):
-        rows = finish(1, s, x[s], *routed[s])
-        ref = out_a if s == 0 else out_b
-        for q in range(QUARTERS):
-            ref[0, :, q * quarter : (q + 1) * quarter] = rows[q].astype(bf16)
+    last(0)
+    last(1)
     out_load[...] = mass_take(4)[:, 0:4] / (2 * TICKS * 8 * 32)
 
     for s in range(2):
@@ -389,7 +438,9 @@
         drain(xr.at[s], send.at[0, s, RELAY])
         for t in range(TICKS):
             drain(rx.at[t, s, blocks(0, 3 + t)], send.at[t, s, TO_OWN])
-            for kind in (TO_OTHER, ON_OWN, ON_OTHER, SWAP_OWN, SWAP_OTHER):
+            for kind in (TO_OTHER, TO_OTHER_FAR):
+                drain(rx.at[t, s, blocks(0, 2)], send.at[t, s, kind])
+            for kind in (ON_OWN, ON_OTHER, SWAP_OWN, SWAP_OTHER):
                 drain(rx.at[t, s, blocks(0, 4)], send.at[t, s, kind])
             drain(home_rx.at[t, s, blocks(0, 7)], send.at[t, s, HOME])
 

time: 95.5 us -> 94.4 us (0.988)
  the two profiles are of different devices: /device:TPU:24 before, /device:TPU:48 now
where the time goes in v4:
time: 94.4 us; the launch traced here: 94.2 us
  Pallas kernels  93.6 us (99%)
    pallas_call x1, Pallas kernels, shards(): pl.pallas_call(kernel, out_shape=(jax.ShapeDtypeStruct(stream_a.shape, bf...  92.1 us

profile of v4, /device:TPU:48, one launch (start us, length us, event | category | flops | bytes accessed | tf_op | source)
XLA Modules:
  0.0 94.2 jit_solution(1557560656144103316)
XLA Ops:
  0.6 92.1 %relay.1 = (bf16[1,8,3584]{2,1,0:T(8,128)(2,1)}, bf16[1,8,3584]{2,1,0:T(8,128)(2,1)}, f32[16,4]{1,0:T(8,128)}) custom-call(bf16[1,8,3584]{2,1,0:T(8,128)(2,1)} %sa.1, bf16[1,8,3584]{2,1,0:T(8,128)(2,1)} %sb.1, s32[2,2,1,2,8]{4,3,2,1,0:T(2,128)} %bitcast.4, bf16[2,1,4,3584]{3,2,1,0:T(4,128)(2,1)} %bitcast.3, bf16[2,1,3584,128]{3,2,1,0:T(8,128)(2,1)} %up.1, ...), custom_call_target="tpu_custom_call" | custom-call | tf_op jit(solution)/shard_map/relay/pallas_call | solution.py:460
  92.7 1.5 %hand_over.1 = (bf16[1,8,3584]{2,1,0:T(8,128)(2,1)}, bf16[1,8,3584]{2,1,0:T(8,128)(2,1)}, f32[4,16]{1,0:T(4,128)}) custom-call(bf16[1,8,3584]{2,1,0:T(8,128)(2,1)} %get-tuple-element.9.a, bf16[1,8,3584]{2,1,0:T(8,128)(2,1)} %get-tuple-element.10.b, f32[16,4]{1,0:T(8,128)} %get-tuple-element.11.load), custom_call_target="tpu_custom_call" | custom-call | tf_op jit(solution)/shard_map/hand_over/pallas_call | solution.py:509

commit v5 on v4

--- a/solution.py
+++ b/solution.py
@@ -200,6 +200,13 @@
         for plane, kind, base in ((zh, TO_OWN, 0), (1 - zh, TO_OTHER, 4)):
             for k, to in reversed(list(enumerate(targets))):
                 src = block(plane * 2 + to // 4)
+                if base == 0 and k == 0:
+                    over = {"expert": ex + 2 * turn}
+                    if t > 0:
+                        over["pipe"] = ahead if s == 0 else behind
+                    remote(
+                        tx.at[t, s, src], rx.at[t, s, block(8)], t, s, ON_OWN, over
+                    ).start()
                 if t == 0 and base == 0 and k == 0:
                     rx[t, s, block(0)] = tx[t, s, src]
                     continue
@@ -223,8 +230,7 @@
         got = blocks(1, 3) if t == 0 else blocks(0, 4)
         drain(rx.at[t, s, got], recv.at[t, s, TO_OWN + group])
         remote(
-            rx.at[t, s, blocks(group * 4, 4)], rx.at[t, s, blocks(8 + group * 4, 4)],
-            t, s, ON_OWN + group, mate,
+            rx.at[t, s, blocks(1, 3)], rx.at[t, s, blocks(9, 3)], t, s, ON_OWN, mate
         ).start()
 
     def experts(t, s):

time: 94.4 us -> 94.5 us (level)
  the two profiles are of different devices: /device:TPU:48 before, /device:TPU:8 now
where the time goes in v5:
time: 94.5 us; the launch traced here: 94.4 us
  Pallas kernels  93.7 us (99%)
    pallas_call x1, Pallas kernels, shards(): pl.pallas_call(kernel, out_shape=(jax.ShapeDtypeStruct(stream_a.shape, bf...  92.2 us

profile of v5, /device:TPU:8, one launch (start us, length us, event | category | flops | bytes accessed | tf_op | source)
XLA Modules:
  0.0 94.4 jit_solution(1948213707912393398)
XLA Ops:
  0.6 92.2 %relay.1 = (bf16[1,8,3584]{2,1,0:T(8,128)(2,1)}, bf16[1,8,3584]{2,1,0:T(8,128)(2,1)}, f32[16,4]{1,0:T(8,128)}) custom-call(bf16[1,8,3584]{2,1,0:T(8,128)(2,1)} %sa.1, bf16[1,8,3584]{2,1,0:T(8,128)(2,1)} %sb.1, s32[2,2,1,2,8]{4,3,2,1,0:T(2,128)} %bitcast.4, bf16[2,1,4,3584]{3,2,1,0:T(4,128)(2,1)} %bitcast.3, bf16[2,1,3584,128]{3,2,1,0:T(8,128)(2,1)} %up.1, ...), custom_call_target="tpu_custom_call" | custom-call | tf_op jit(solution)/shard_map/relay/pallas_call | solution.py:466
  92.9 1.5 %hand_over.1 = (bf16[1,8,3584]{2,1,0:T(8,128)(2,1)}, bf16[1,8,3584]{2,1,0:T(8,128)(2,1)}, f32[4,16]{1,0:T(4,128)}) custom-call(bf16[1,8,3584]{2,1,0:T(8,128)(2,1)} %get-tuple-element.9.a, bf16[1,8,3584]{2,1,0:T(8,128)(2,1)} %get-tuple-element.10.b, f32[16,4]{1,0:T(8,128)} %get-tuple-element.11.load), custom_call_target="tpu_custom_call" | custom-call | tf_op jit(solution)/shard_map/hand_over/pallas_call | solution.py:515
